TPU v7x, 128 devices: a whole 4x4x4 slice. The times are simulated.
128 devices in a mesh: seq: 16 (over y, z), expert: 8 (over x, core).
Axes of the slice: x: 4, y: 4, z: 4, core: 2. Of those that a mesh axis runs over, the one named last changes fastest.
Arguments:
- tokens: bfloat16 [8, 4096, 1152], P('expert', 'seq'), may hold values from -6 to 6
- expert_index: int32 [8, 4096, 1], P('expert', 'seq'), may hold values from 0 to 7; in each aligned block of 256 rows (0 to 255, 256 to 511, ..., all dimensions but the last counted through in order) at most 64 rows name the same one
- cotangent: bfloat16 [8, 4096, 1152], P('expert', 'seq'), may hold values from -6 to 6
- first_gain: float32 [1152], replicated, may hold values from 0.5 to 1.5
- in_weight: bfloat16 [1152, 4608], replicated, may hold values from -0.1875 to 0.1875
- conv_weight: float32 [4, 2304], replicated, may hold values from -3 to 3
- conv_bias: float32 [2304], replicated, may hold values from -3 to 3
- select_weight: bfloat16 [2304, 104], replicated, may hold values from -0.125 to 0.125
- step_weight: bfloat16 [72, 2304], replicated, may hold values from -0.75 to 0.75
- step_bias: float32 [2304], replicated, may hold values from -4 to -2.5
- decay_log: float32 [16, 2304], replicated, may hold values from -9 to 1
- skip_gain: float32 [2304], replicated, may hold values from 0.5 to 1.5
- out_weight: bfloat16 [2304, 1152], replicated, may hold values from -0.125 to 0.125
- second_gain: float32 [1152], replicated, may hold values from 0.5 to 1.5
- router_weight: bfloat16 [1152, 8], replicated, may hold values from -0.125 to 0.125
- expert_first: bfloat16 [8, 1152, 3072], P('expert'), may hold values from -0.1875 to 0.1875
- expert_second: bfloat16 [8, 3072, 1152], P('expert'), may hold values from -0.875 to 0.875
Outputs:
- mixed: bfloat16 [8, 4096, 1152], P('expert', 'seq')
- grad_tokens: float32 [8, 4096, 1152], P('expert', 'seq')
- grad_first_gain: float32 [1152], P(('seq', 'expert'))
- grad_in_weight: float32 [1152, 4608], P(None, ('seq', 'expert'))
- grad_conv_weight: float32 [4, 2304], P(None, ('seq', 'expert'))
- grad_conv_bias: float32 [2304], P(('seq', 'expert'))
- grad_select_weight: float32 [2304, 104], P(('seq', 'expert'))
- grad_step_weight: float32 [72, 2304], P(None, ('seq', 'expert'))
- grad_step_bias: float32 [2304], P(('seq', 'expert'))
- grad_decay_log: float32 [16, 2304], P(None, ('seq', 'expert'))
- grad_skip_gain: float32 [2304], P(('seq', 'expert'))
- grad_out_weight: float32 [2304, 1152], P(('seq', 'expert'))
- grad_second_gain: float32 [1152], P(('seq', 'expert'))
- grad_router_weight: float32 [1152, 8], P(('seq', 'expert'))
- grad_expert_first: float32 [8, 1152, 3072], P('expert', None, 'seq')
- grad_expert_second: float32 [8, 3072, 1152], P('expert', 'seq')
Inputs may be any that keep to these rules, and one draw needn't show every extreme that they name: `expert_index`: in each aligned block of 256 tokens of a sequence no expert is named more than 64 times, a bound that some block reaches.
All inputs are finite; a program needn't handle non-finite values.
Results may differ from a plain program's by a relative error of at most 0.038.
Values may be sent and summed in bfloat16 or wider, within the bound.
A program may use at most 256 MiB of HBM per device.

v0:
```python
import functools
import math

import jax
import jax.numpy as jnp
from jax import lax
from jax.experimental import pallas as pl
from jax.experimental.pallas import tpu as pltpu
from jax.sharding import PartitionSpec as P

LANES = 128
SEGS = 8
LOG2E = math.log2(math.e)
PARTS = 3
SELECTED = 104
EXPERTS = 8
CAPACITY = 64
CUT = 768
GRID = 4


def spread_ones(states):
    row = lax.broadcasted_iota(jnp.int32, (LANES, states * LANES), 0)
    lane = lax.broadcasted_iota(jnp.int32, (LANES, states * LANES), 1)
    return row, lane // LANES


def fill_maps(sel_ref, wide_ref, column):
    steps, states = wide_ref.shape[:2]
    row, block = spread_ones(states)
    ones = jnp.where(row == block + column, 1.0, 0.0).astype(jnp.bfloat16)
    left, total = sel_ref[...], None
    for unused in range(3):
        part = left.astype(jnp.bfloat16)
        left = left - part.astype(jnp.float32)
        spread = jnp.dot(part, ones, preferred_element_type=jnp.float32)
        total = spread if total is None else total + spread
    for n in range(states):
        wide_ref[:, n] = total[:, n * LANES : (n + 1) * LANES].reshape(steps, SEGS, LANES)


def gather_maps(sum_ref, column):
    steps, states = sum_ref.shape[:2]
    row, block = spread_ones(states)
    ones = jnp.where(row == block + column, 1.0, 0.0).astype(jnp.bfloat16)
    left = jnp.concatenate([sum_ref[:, n].reshape(steps * SEGS, LANES) for n in range(states)], axis=1)
    total = None
    for unused in range(3):
        part = left.astype(jnp.bfloat16)
        left = left - part.astype(jnp.float32)
        summed = transposed_dot(part, ones)
        total = summed if total is None else total + summed
    return total


def lanes_of(block):
    return pl.ds(pl.multiple_of(block * LANES, LANES), LANES)


def rows_of(j):
    return pl.ds(pl.multiple_of(j * SEGS, SEGS), SEGS)


def rates_of(log_ref, lanes):
    states = log_ref.shape[0]
    rate = -LOG2E * jnp.exp(log_ref[:, lanes])
    return jnp.stack([jnp.broadcast_to(rate[n : n + 1], (SEGS, LANES)) for n in range(states)])


def neighbour(value, hop, later, fill):
    axis = value.ndim - 2
    place = lax.broadcasted_iota(jnp.int32, value.shape, axis)
    if later:
        return jnp.where(place < SEGS - hop, pltpu.roll(value, SEGS - hop, axis), fill)
    return jnp.where(place >= hop, pltpu.roll(value, hop, axis), fill)


def summarize(later, part, step_ref, other_ref, wide, log_ref, part_ref, span_ref, message):
    steps, states = wide.shape[:2]
    blocks = step_ref.shape[1] // LANES // PARTS

    def block(i, unused):
        lanes = lanes_of(part * blocks + i)
        rate = rates_of(log_ref, lanes)

        def advance(turn, carry):
            span, memory = carry
            j = steps - 1 - turn if later else turn
            step = step_ref[rows_of(j), lanes]
            other = other_ref[rows_of(j), lanes]
            decay = jnp.exp2(step * rate)
            if later:
                memory = decay * (memory + wide[j] * other)
            else:
                memory = decay * memory + wide[j] * (step * other)
            return span + step, memory

        zero = jnp.zeros((SEGS, LANES), jnp.float32)
        span, memory = lax.fori_loop(0, steps, advance, (zero, jnp.zeros(rate.shape, jnp.float32)), unroll=8)
        hop = 1
        while hop < SEGS:
            memory = memory + jnp.exp2(rate * span) * neighbour(memory, hop, later, 0.0)
            span = span + neighbour(span, hop, later, 0.0)
            hop *= 2
        span_ref[:, lanes] = span
        part_ref[:, :, lanes] = memory
        end = 0 if later else SEGS - 1
        for n in range(states):
            message[n // GRID, n % GRID, pl.ds(i, 1), :] = memory[n, end : end + 1]
        for q in range(GRID):
            message[q, GRID, pl.ds(i, 1), :] = span[end : end + 1]
        return unused

    lax.fori_loop(0, blocks, block, 0)


def entering(later, part_ref, span_ref, rate, lanes, carried):
    ends = part_ref[:, :, lanes] + jnp.exp2(rate * span_ref[:, lanes]) * carried
    return neighbour(ends, 1, later, carried)


def carried_at(in_ref, part, i):
    states = GRID * GRID
    return jnp.stack(
        [jnp.broadcast_to(in_ref[n // GRID, n % GRID, pl.ds(i, 1), :], (SEGS, LANES)) for n in range(states)]
    )


def scan_part(part, step_ref, conv_ref, wide_in, wide_out, log_ref, part_ref, span_ref, in_ref, y_ref, entry_ref):
    steps = wide_in.shape[0]
    blocks = step_ref.shape[1] // LANES // PARTS

    def block(i, unused):
        lanes = lanes_of(part * blocks + i)
        rate = rates_of(log_ref, lanes)
        first = entering(False, part_ref, span_ref, rate, lanes, carried_at(in_ref, part, i))
        entry_ref[:, :, lanes] = first

        def advance(j, memory):
            step = step_ref[rows_of(j), lanes]
            memory = jnp.exp2(step * rate) * memory + wide_in[j] * (step * conv_ref[rows_of(j), lanes])
            y_ref[rows_of(j), lanes] = jnp.sum(wide_out[j] * memory, axis=0)
            return memory

        lax.fori_loop(0, steps, advance, first, unroll=8)
        return unused

    lax.fori_loop(0, blocks, block, 0)


def retreat_part(
    part, step_ref, conv_ref, grad_ref, raw_ref, wide_in, wide_out, log_ref, pull_ref, entry_ref, part_ref, span_ref, in_ref,
    low_ref, gconv_ref, glog_ref, gbias_ref, sum_in, sum_out, states_ref, decays_ref, raw_sum, raw_rows,
):
    steps = wide_in.shape[0]
    blocks = step_ref.shape[1] // LANES // PARTS

    def block(i, unused):
        lanes = lanes_of(part * blocks + i)
        rate = rates_of(log_ref, lanes)

        def advance(j, memory):
            step = step_ref[rows_of(j), lanes]
            decay = jnp.exp2(step * rate)
            memory = decay * memory + wide_in[j] * (step * conv_ref[rows_of(j), lanes])
            decays_ref[j] = decay
            states_ref[j + 1] = memory
            return memory

        first = entry_ref[:, :, lanes]
        states_ref[0] = first
        lax.fori_loop(0, steps, advance, first, unroll=8)

        def retreat(turn, carry):
            j = steps - 1 - turn
            mu, slow = carry
            step = step_ref[rows_of(j), lanes]
            conv = conv_ref[rows_of(j), lanes]
            grad = grad_ref[rows_of(j), lanes]
            lam = wide_out[j] * grad + mu
            sum_out[j] += grad * states_ref[j + 1]
            sum_in[j] += lam * (step * conv)
            by_in = jnp.sum(lam * wide_in[j], axis=0)
            mu = lam * decays_ref[j]
            kept = mu * states_ref[j]
            by_rate = jnp.sum(kept * rate, axis=0)
            grad_step = by_in * conv + (1.0 / LOG2E) * by_rate
            raw_rows[rows_of(j), :] = grad_step * jax.nn.sigmoid(raw_ref[rows_of(j), lanes])
            gconv_ref[rows_of(j), lanes] = by_in * step
            return mu, slow + kept * step

        last = entering(True, part_ref, span_ref, rate, lanes, carried_at(in_ref, part, i))
        unused_mu, slow = lax.fori_loop(0, steps, retreat, (last, jnp.zeros(rate.shape, jnp.float32)), unroll=4)
        glog_ref[:, lanes] = (1.0 / LOG2E) * jnp.sum(slow * rate, axis=1)
        raw_steps = raw_rows[...]
        gbias_ref[:, lanes] = jnp.sum(raw_steps, axis=0, keepdims=True)
        low = raw_steps.astype(jnp.bfloat16)
        low_ref[:, lanes] = low
        raw_sum[:, : pull_ref.shape[0]] += transposed_dot(low, pull_ref[:, lanes])
        return unused

    lax.fori_loop(0, blocks, block, 0)


class Relay:
    def __init__(self, later, log_ref, log_rows, in_ref, message, got, row, rows_got, above, made, sends, arrivals, chained=False):
        self.later, self.log_rows, self.message, self.got = later, log_rows, message, got
        self.row, self.rows_got, self.above, self.made, self.in_ref = row, rows_got, above, made, in_ref
        self.sends, self.arrivals = sends, arrivals
        seq = lax.axis_index("seq")
        self.y, self.z = lax.div(seq, GRID), lax.rem(seq, GRID)
        blocks = log_ref.shape[1] // LANES // PARTS
        log_rows[...] = jnp.zeros_like(log_rows)
        for part in range(PARTS):
            for b in range(blocks):
                lanes = pl.ds((part * blocks + b) * LANES, LANES)
                for n in range(GRID * GRID):
                    log_rows[part, n // GRID, n % GRID, b : b + 1, :] = log_ref[n : n + 1, lanes]
        self.flying = {}
        barrier = pltpu.get_barrier_semaphore()
        peers = [self.across(k) for k in range(1, GRID)] + [self.along(k) for k in range(1, GRID)]
        if chained:
            peers += [self.onward(1), self.onward(-1)]
        for peer in peers:
            pl.semaphore_signal(barrier, inc=1, device_id=peer, device_id_type=pl.DeviceIdType.MESH)
        self.peers = len(peers)

    def onward(self, k):
        size = GRID * GRID
        return {"seq": lax.rem(self.y * GRID + self.z + k + size, size)}

    def across(self, k):
        return {"seq": self.y * GRID + lax.rem(self.z + k, GRID)}

    def along(self, k):
        return {"seq": lax.rem(self.y + k, GRID) * GRID + self.z}

    def meet(self):
        pl.semaphore_wait(pltpu.get_barrier_semaphore(), self.peers)

    def send(self, part, phase, k, source, target, peer):
        copy = pltpu.make_async_remote_copy(
            src_ref=source, dst_ref=target, send_sem=self.sends.at[part, phase, k], recv_sem=self.arrivals.at[part, phase, k],
            device_id=peer, device_id_type=pl.DeviceIdType.MESH,
        )
        copy.start()
        self.flying.setdefault((part, phase), []).append(copy)

    def land(self, part, phase):
        for copy in self.flying[part, phase]:
            copy.wait()

    def order(self):
        return range(GRID - 1, -1, -1) if self.later else range(GRID)

    def rate(self, part):
        return -LOG2E * jnp.exp(self.log_rows[part, self.z])

    def first(self, part):
        for k in range(1, GRID):
            peer = lax.rem(self.z + k, GRID)
            self.send(part, 0, k, self.message.at[part, peer], self.got.at[part, k], self.across(k))
        self.got[part, 0] = self.message[part, self.z]

    def second(self, part):
        self.land(part, 0)
        rate = self.rate(part)
        state, span = jnp.zeros(rate.shape, jnp.float32), jnp.zeros(rate.shape[1:], jnp.float32)
        for z in self.order():
            block = self.got[part, lax.rem(self.z - z + GRID, GRID)]
            state = jnp.exp2(rate * block[GRID]) * state + block[:GRID]
            span = span + block[GRID]
        self.row[part, :GRID] = state
        self.row[part, GRID] = span
        for k in range(1, GRID):
            self.send(part, 1, k, self.row.at[part], self.rows_got.at[part, k], self.along(k))
        self.rows_got[part, 0] = self.row[part]

    def third(self, part):
        self.land(part, 1)
        rate = self.rate(part)
        state = jnp.zeros(rate.shape, jnp.float32)
        for y in self.order():
            self.above[part, y] = state
            block = self.rows_got[part, lax.rem(self.y - y + GRID, GRID)]
            state = jnp.exp2(rate * block[GRID]) * state + block[:GRID]
        state = self.above[part, self.y]
        for z in self.order():
            self.made[part, z] = state
            block = self.got[part, lax.rem(self.z - z + GRID, GRID)]
            state = jnp.exp2(rate * block[GRID]) * state + block[:GRID]
        for k in range(1, GRID):
            peer = lax.rem(self.z + k, GRID)
            self.send(part, 2, k, self.made.at[part, peer], self.in_ref.at[part, self.z], self.across(k))
        self.in_ref[part, self.z] = self.made[part, self.z]

    def done(self, part):
        self.land(part, 2)


def staged(relay, summary, extra, scan):
    summary(0)
    relay.first(0)
    summary(1)
    relay.first(1)
    relay.second(0)
    summary(2)
    relay.first(2)
    relay.third(0)
    relay.second(1)
    extra()
    relay.second(2)
    relay.third(1)
    relay.done(0)
    scan(0)
    relay.third(2)
    relay.done(1)
    scan(1)
    relay.done(2)
    scan(2)


def named_experts(slot_ref, rows):
    slot = slot_ref[...]
    first = lax.broadcasted_iota(jnp.int32, (rows, EXPERTS), 1) * CAPACITY
    return jnp.where((slot >= first) & (slot < first + CAPACITY), 1.0, 0.0)


def seated_rows(slot_ref, rows, seats):
    return jnp.where(lax.broadcasted_iota(jnp.int32, (rows, seats), 1) == slot_ref[...], 1.0, 0.0).astype(jnp.bfloat16)


def mixer_kernel(
    token_ref, row_ref, in_hbm, tap_ref, select_ref, step_weight_ref, log_ref, out_hbm, router_ref, slot_ref,
    normed_out, gate_out, padded_out, pre_out, conv_out, raw_out, step_out, sel_out, entry_out, mixer_out, gated_out,
    middle_out, normed_mid_out, probs_out, chosen_out, leaving_out,
    normed, in_ref, out_ref, padded, gate, pre, conv, raw, step, sel, entry, mixer, gated, middle, normed_mid, probs, chosen, leaving,
    tail, tail_got, part_ref, span_ref, wide_in, wide_out, loads, saves, passing, log_rows, relay_in, *relayed
):
    rows, width = step.shape
    model = token_ref.shape[1]
    tap_bias_ref, step_bias_ref, skip_ref = (row_ref.at[k : k + 1] for k in range(3))
    gain_ref, second_gain_ref = row_ref.at[3:4, :model], row_ref.at[3:4, model:]
    taps, states = tap_ref.shape[0], log_ref.shape[0]
    reach = (taps - 1) * SEGS
    rank = SELECTED - 2 * states
    pieces = in_ref.shape[0]
    cut = in_ref.shape[2]
    blocks = width // LANES

    loading = [pltpu.make_async_copy(in_hbm.at[:, pl.ds(k * cut, cut)], in_ref.at[k], loads.at[k]) for k in range(pieces)]
    loading.append(pltpu.make_async_copy(out_hbm, out_ref, loads.at[pieces]))
    for copy in loading:
        copy.start()
    saving = []

    def save(source, target):
        copy = pltpu.make_async_copy(source, target, saves.at[len(saving)])
        copy.start()
        saving.append(copy)

    relay = Relay(False, log_ref, log_rows, relay_in, *relayed, chained=True)

    stream = token_ref[...].astype(jnp.float32)
    normed[...] = (stream * rms_scale(stream) * gain_ref[...]).astype(jnp.bfloat16)
    save(normed, normed_out)
    for k in range(pieces // 2):
        loading[k].wait()
        padded[reach:, k * cut : (k + 1) * cut] = jnp.dot(normed[...], in_ref[k], preferred_element_type=jnp.float32)
    tail[...] = jnp.zeros_like(tail)
    for k in range(taps - 1):
        row = reach + rows - (taps - 1 - k) * SEGS + SEGS - 1
        tail[k : k + 1, :] = padded[row : row + 1, :]
    relay.meet()
    handing = pltpu.make_async_remote_copy(
        src_ref=tail, dst_ref=tail_got, send_sem=passing.at[0], recv_sem=passing.at[1],
        device_id=relay.onward(1), device_id_type=pl.DeviceIdType.MESH,
    )
    handing.start()
    for k in range(pieces // 2, pieces):
        loading[k].wait()
        spot = slice((k - pieces // 2) * cut, (k - pieces // 2 + 1) * cut)
        gate[:, spot] = jnp.dot(normed[...], in_ref[k], preferred_element_type=jnp.float32)
    save(gate, gate_out)
    handing.wait()
    started = jnp.where(lax.axis_index("seq") > 0, 1.0, 0.0)
    for k in range(taps - 1):
        row = rows + k * SEGS
        segment = lax.broadcasted_iota(jnp.int32, (SEGS, width), 0)
        before = pltpu.roll(padded[row : row + SEGS, :], 1, 0)
        padded[k * SEGS : (k + 1) * SEGS, :] = jnp.where(segment == 0, started * tail_got[k : k + 1, :], before)
    save(padded, padded_out)

    sel[...] = jnp.zeros_like(sel)

    def convolve(b, unused):
        lanes = lanes_of(b)
        value = tap_bias_ref[:, lanes]
        for k in range(taps):
            value = value + tap_ref[k : k + 1, lanes] * padded[k * SEGS : k * SEGS + rows, lanes]
        pre[:, lanes] = value
        value = value * jax.nn.sigmoid(value)
        conv[:, lanes] = value
        sel[:, :SELECTED] += jnp.dot(value.astype(jnp.bfloat16), select_ref[lanes, :], preferred_element_type=jnp.float32)
        return unused

    lax.fori_loop(0, blocks, convolve, 0)
    save(pre, pre_out)
    save(conv, conv_out)
    save(sel, sel_out)
    step_low = sel[:, :rank].astype(jnp.bfloat16)

    def size(b, unused):
        lanes = lanes_of(b)
        value = jnp.dot(step_low, step_weight_ref[:, lanes], preferred_element_type=jnp.float32) + step_bias_ref[:, lanes]
        raw[:, lanes] = value
        step[:, lanes] = jnp.maximum(value, 0.0) + jnp.log1p(jnp.exp(-jnp.abs(value)))
        return unused

    lax.fori_loop(0, blocks, size, 0)
    save(raw, raw_out)
    save(step, step_out)
    fill_maps(sel, wide_in, rank)

    def summary(part):
        summarize(False, part, step, conv, wide_in, log_ref, part_ref, span_ref, relay.message.at[part])

    def scan(part):
        scan_part(part, step, conv, wide_in, wide_out, log_ref, part_ref, span_ref, relay_in.at[part], mixer, entry)

    staged(relay, summary, lambda: fill_maps(sel, wide_out, rank + states), scan)
    save(entry, entry_out)

    def blend(b, unused):
        lanes = lanes_of(b)
        value = mixer[:, lanes] + skip_ref[:, lanes] * conv[:, lanes]
        mixer[:, lanes] = value
        opening = gate[:, lanes]
        gated[:, lanes] = (value * (opening * jax.nn.sigmoid(opening))).astype(jnp.bfloat16)
        return unused

    lax.fori_loop(0, blocks, blend, 0)
    save(mixer, mixer_out)
    save(gated, gated_out)
    loading[pieces].wait()
    value = token_ref[...].astype(jnp.float32) + jnp.dot(gated[...], out_ref[...], preferred_element_type=jnp.float32)
    middle[...] = value
    save(middle, middle_out)
    normed_mid[...] = (value * rms_scale(value) * second_gain_ref[...]).astype(jnp.bfloat16)
    save(normed_mid, normed_mid_out)
    logits = jnp.dot(normed_mid[...], router_ref[...], preferred_element_type=jnp.float32)
    grown = jnp.exp(logits - jnp.max(logits, axis=1, keepdims=True))
    probs[...] = grown / jnp.sum(grown, axis=1, keepdims=True)
    save(probs, probs_out)
    gate_value = jnp.sum(named_experts(slot_ref, rows) * probs[...], axis=1, keepdims=True)
    chosen[...] = jnp.broadcast_to(gate_value, (rows, LANES))
    save(chosen, chosen_out)
    place = lax.broadcasted_iota(jnp.int32, (rows, LANES), 1)
    parts = jnp.zeros((rows, LANES), jnp.float32)
    for k, piece in enumerate(three_parts(gate_value)):
        parts = jnp.where(place == k, piece.astype(jnp.float32), parts)
    seating = seated_rows(slot_ref, rows, leaving.shape[0])
    leaving[:, :model] = column_dot(seating, normed_mid[...]).astype(jnp.bfloat16)
    leaving[:, model:] = column_dot(seating, parts.astype(jnp.bfloat16)).astype(jnp.bfloat16)
    save(leaving, leaving_out)
    for copy in saving:
        copy.wait()


def mixer_back_kernel(
    back_hbm, slot_ref, probs_ref, chosen_ref, normed_ref, router_ref, middle_ref, up_ref, out_hbm, gate_hbm,
    mixer_hbm, conv_hbm, step_hbm, raw_hbm, sel_ref, pre_hbm, padded_hbm, entry_hbm, log_ref, step_weight_ref, select_ref,
    tap_ref, packed_ref, in_hbm, token_ref,
    low_out, gate_out, conv_out, left_out, right_out, narrow_out, token_out,
    back, out_ref, gate, mixer, conv, step, raw, padded, entry, in_ref,
    middle_low, grad_gate, grad_conv, left, right, narrow, grad_middle, mixed, low, gsel, glog, gbias, total, tail, tail_got, row_ref,
    part_ref, span_ref, wide_in, wide_out, sum_in, sum_out, states_ref, decays_ref, raw_sum, raw_rows,
    loads, saves, passing, log_rows, relay_in, *relayed
):
    rows, width = step.shape
    model = up_ref.shape[1]
    skip_ref, gain_ref, second_gain_ref = packed_ref.at[2:3], packed_ref.at[3:4, :model], packed_ref.at[3:4, model:]
    taps, states = tap_ref.shape[0], log_ref.shape[0]
    rank = SELECTED - 2 * states
    held, cut = in_ref.shape[0], in_ref.shape[2]
    blocks = width // LANES
    saving, numbers = [], iter(range(64))

    def load(source, target):
        copy = pltpu.make_async_copy(source, target, loads.at[next(numbers)])
        copy.start()
        return copy

    def save(source, target):
        copy = pltpu.make_async_copy(source, target, saves.at[len(saving)])
        copy.start()
        saving.append(copy)

    def weight(k):
        return load(in_hbm.at[:, pl.ds(k * cut, cut)], in_ref.at[k % held])

    early = [load(back_hbm, back), load(out_hbm, out_ref), load(gate_hbm, gate), load(mixer_hbm, mixer)]
    scanning = [load(step_hbm, step), load(conv_hbm, conv), load(raw_hbm, raw), load(entry_hbm, entry)]
    padding = load(padded_hbm, padded)
    weights = {k: weight(k) for k in range(held, 2 * held)}
    relay = Relay(True, log_ref, log_rows, relay_in, *relayed, chained=True)

    early[0].wait()
    seating = seated_rows(slot_ref, rows, back.shape[0])
    chosen = chosen_ref[:, 0:1]
    along = jnp.sum(jnp.dot(seating, back[:, model:], preferred_element_type=jnp.float32), axis=1, keepdims=True)
    place = lax.broadcasted_iota(jnp.int32, (rows, LANES), 1)
    logits = (along * chosen * (named_experts(slot_ref, rows) - probs_ref[...])).astype(jnp.bfloat16)
    grad = transposed_dot(logits, router_ref[...]) + chosen * jnp.dot(seating, back[:, :model], preferred_element_type=jnp.float32)
    narrow[...] = jnp.zeros_like(narrow)
    narrow[2 : 2 + EXPERTS, :] = column_dot(logits, normed_ref[...])
    value = middle_ref[...]
    returned, gained = rms_back(value, rms_scale(value), second_gain_ref[...], grad)
    narrow[1:2, :] = gained[None, :]
    value = up_ref[...].astype(jnp.float32) + returned
    grad_middle[...] = value
    middle_low[...] = value.astype(jnp.bfloat16)
    save(middle_low, low_out)
    for copy in early[1:]:
        copy.wait()

    def open_gate(b, unused):
        lanes = lanes_of(b)
        grown = transposed_dot(middle_low[...], out_ref[lanes, :])
        opening = gate[:, lanes]
        mixed[:, lanes] = grown * (opening * jax.nn.sigmoid(opening))
        grad_gate[:, lanes] = (grown * mixer[:, lanes] * silu_slope(opening)).astype(jnp.bfloat16)
        return unused

    lax.fori_loop(0, blocks, open_gate, 0)
    save(grad_gate, gate_out)
    pre, gconv = gate, mixer
    activating = load(pre_hbm, pre)
    for copy in scanning:
        copy.wait()

    fill_maps(sel_ref, wide_out, rank + states)

    def summary(part):
        summarize(True, part, step, mixed, wide_out, log_ref, part_ref, span_ref, relay.message.at[part])

    def prepare():
        fill_maps(sel_ref, wide_in, rank)
        sum_in[...] = jnp.zeros_like(sum_in)
        sum_out[...] = jnp.zeros_like(sum_out)
        raw_sum[...] = jnp.zeros_like(raw_sum)

    def scan(part):
        retreat_part(
            part, step, conv, mixed, raw, wide_in, wide_out, log_ref, step_weight_ref, entry, part_ref, span_ref,
            relay_in.at[part], low, gconv, glog, gbias, sum_in, sum_out, states_ref, decays_ref, raw_sum, raw_rows,
        )

    relay.meet()
    staged(relay, summary, prepare, scan)
    maps = gather_maps(sum_in, rank) + gather_maps(sum_out, rank + states)
    gsel[...] = (raw_sum[...] + maps).astype(jnp.bfloat16)

    activating.wait()
    padding.wait()
    step_low = jnp.where(place < rank, sel_ref[...], 0.0).astype(jnp.bfloat16)
    tall = lax.broadcasted_iota(jnp.int32, (row_ref.shape[0], LANES), 0)
    spots = jnp.where(lax.broadcasted_iota(jnp.int32, tall.shape, 1) == tall + SELECTED, 1.0, 0.0).astype(jnp.bfloat16)
    row_ref[...] = jnp.zeros_like(row_ref)

    def convolve_back(b, unused):
        lanes = lanes_of(b)
        around, kept = mixed[:, lanes], conv[:, lanes]
        grown = transposed_dot(gsel[:, :SELECTED], select_ref[lanes, :]) + gconv[:, lanes] + skip_ref[:, lanes] * around
        grown = grown * silu_slope(pre[:, lanes])
        gconv[:, lanes] = grown
        row_ref[:states, :] = glog[:, lanes]
        for k in range(taps):
            row_ref[states + k : states + k + 1, :] = jnp.sum(
                grown * padded[k * SEGS : k * SEGS + rows, lanes], axis=0, keepdims=True
            )
        row_ref[states + taps : states + taps + 1, :] = jnp.sum(grown, axis=0, keepdims=True)
        row_ref[states + taps + 1 : states + taps + 2, :] = gbias[:, lanes]
        row_ref[states + taps + 2 : states + taps + 3, :] = jnp.sum(around * kept, axis=0, keepdims=True)
        summed = column_dot(kept.astype(jnp.bfloat16), gsel[...])
        for piece in three_parts(row_ref[...]):
            summed = summed + column_dot(piece, spots)
        left[lanes, :] = summed
        right[lanes, :] = column_dot(low[:, lanes], step_low)
        return unused

    lax.fori_loop(0, blocks, convolve_back, 0)
    save(left, left_out)
    save(right, right_out)

    tail[...] = jnp.zeros_like(tail)
    for k in range(taps - 1):
        tail[k : k + 1, :] = gconv[k * SEGS : k * SEGS + 1, :]
    handing = pltpu.make_async_remote_copy(
        src_ref=tail, dst_ref=tail_got, send_sem=passing.at[0], recv_sem=passing.at[1],
        device_id=relay.onward(-1), device_id_type=pl.DeviceIdType.MESH,
    )
    handing.start()
    for k in range(held):
        weights[held + k].wait()
        summed = transposed_dot(grad_gate[:, k * cut : (k + 1) * cut], in_ref[k])
        total[...] = summed if k == 0 else total[...] + summed
        weights[k] = weight(k)
    handing.wait()
    goes_on = jnp.where(lax.axis_index("seq") < GRID * GRID - 1, 1.0, 0.0)
    segment = lax.broadcasted_iota(jnp.int32, (SEGS, cut), 0)
    for k in range(held):
        spot = slice(k * cut, (k + 1) * cut)
        grown = None
        for t in range(taps):
            late = taps - 1 - t
            shifted = gconv[late * SEGS :, spot]
            if late:
                wrapped = [
                    jnp.where(
                        segment == SEGS - 1,
                        goes_on * tail_got[j : j + 1, spot],
                        pltpu.roll(gconv[j * SEGS : (j + 1) * SEGS, spot], SEGS - 1, 0),
                    )
                    for j in range(late)
                ]
                shifted = jnp.concatenate([shifted] + wrapped, axis=0)
            term = tap_ref[t : t + 1, spot] * shifted
            grown = term if grown is None else grown + term
        grad_conv[:, spot] = grown.astype(jnp.bfloat16)
        weights[k].wait()
        total[...] += transposed_dot(grad_conv[:, spot], in_ref[k])
    save(grad_conv, conv_out)
    stream = token_ref[...].astype(jnp.float32)
    returned, gained = rms_back(stream, rms_scale(stream), gain_ref[...], total[...])
    narrow[0:1, :] = gained[None, :]
    total[...] = grad_middle[...] + returned
    save(narrow, narrow_out)
    save(total, token_out)
    for copy in saving:
        copy.wait()


WHOLE = pl.BlockSpec(memory_space=pltpu.VMEM)


def shaped(*dims, dtype=jnp.float32):
    return jax.ShapeDtypeStruct(dims, dtype)


def roomy(mebibytes, **more):
    return pltpu.CompilerParams(vmem_limit_bytes=mebibytes << 20, **more)


def busy(elements):
    return pl.CostEstimate(flops=4096 * elements, bytes_accessed=16 * elements, transcendentals=4 * elements)


def wide_scratch(rows, states, extra=0):
    return pltpu.VMEM((rows // SEGS + extra, states, SEGS, LANES), jnp.float32)


def chain_scratch(states, width):
    return [pltpu.VMEM((states, SEGS, width), jnp.float32), pltpu.VMEM((SEGS, width), jnp.float32)]


def relay_scratch():
    def kept(*dims):
        return pltpu.VMEM((PARTS,) + dims + (SEGS, LANES), jnp.float32)

    return [
        kept(GRID, GRID),
        kept(GRID, GRID),
        kept(GRID, GRID + 1),
        kept(GRID, GRID + 1),
        kept(GRID + 1),
        kept(GRID, GRID + 1),
        kept(GRID, GRID),
        kept(GRID, GRID),
        pltpu.SemaphoreType.DMA((PARTS, 3, GRID)),
        pltpu.SemaphoreType.DMA((PARTS, 3, GRID)),
    ]


def mixer(tokens, packed, in_weight, taps, select, step_weight, decay_log, out_weight, router, slots, seats):
    rows, model = tokens.shape
    states, width = decay_log.shape
    reach = (taps.shape[0] - 1) * SEGS
    bf16, f32 = jnp.bfloat16, jnp.float32
    anywhere = pl.BlockSpec(memory_space=pl.ANY)
    results = [
        ((rows, model), bf16),
        ((rows, width), f32),
        ((rows + reach, width), f32),
        ((rows, width), f32),
        ((rows, width), f32),
        ((rows, width), f32),
        ((rows, width), f32),
        ((rows, LANES), f32),
        ((states, SEGS, width), f32),
        ((rows, width), f32),
        ((rows, width), bf16),
        ((rows, model), f32),
        ((rows, model), bf16),
        ((rows, EXPERTS), f32),
        ((rows, LANES), f32),
        ((seats, model + LANES), bf16),
    ]
    kept = [pltpu.VMEM(dims, dtype) for dims, dtype in results]
    weights = [pltpu.VMEM((2 * width // CUT, model, CUT), bf16), pltpu.VMEM(out_weight.shape, bf16)]
    relayed = relay_scratch()
    return pl.pallas_call(
        mixer_kernel,
        out_shape=tuple(shaped(*dims, dtype=dtype) for dims, dtype in results),
        in_specs=[WHOLE] * 2 + [anywhere] + [WHOLE] * 4 + [anywhere] + [WHOLE] * 2,
        out_specs=(anywhere,) * len(results),
        scratch_shapes=kept[:1]
        + weights
        + [kept[2], kept[1]]
        + kept[3:]
        + [pltpu.VMEM((SEGS, width), f32)] * 2
        + chain_scratch(states, width)
        + [wide_scratch(rows, states)] * 2
        + [
            pltpu.SemaphoreType.DMA((2 * width // CUT + 1,)),
            pltpu.SemaphoreType.DMA((len(results),)),
            pltpu.SemaphoreType.DMA((2,)),
        ]
        + relayed,
        compiler_params=roomy(60, collective_id=0, has_side_effects=True),
        cost_estimate=busy(rows * states * width),
        name="mixer",
    )(tokens, packed, in_weight, taps, select, step_weight, decay_log, out_weight, router, slots)


def mixer_back(
    back, slots, probs, chosen, normed, router, middle, up, out_weight, gate, mixed, conv, step, raw, selection, pre, padded, entry,
    decay_log, step_weight, select, taps, packed, in_weight, tokens,
):
    rows, width = step.shape
    model = tokens.shape[1]
    states = decay_log.shape[0]
    bf16, f32 = jnp.bfloat16, jnp.float32
    anywhere = pl.BlockSpec(memory_space=pl.ANY)
    held = width // CUT
    tall = ((rows, width), f32)
    results = [
        ((rows, model), bf16),
        ((rows, width), bf16),
        ((rows, width), bf16),
        ((width, LANES), f32),
        ((width, LANES), f32),
        ((16, model), f32),
        ((rows, model), f32),
    ]
    streamed = (0, 8, 9, 10, 11, 12, 13, 15, 16, 17, 23)
    kept = (
        [(back.shape, bf16), (out_weight.shape, bf16)]
        + [tall] * 5
        + [(padded.shape, f32), (entry.shape, f32), ((held, model, CUT), bf16)]
        + results[:6]
        + [((rows, model), f32), tall, ((rows, width), bf16), ((rows, LANES), bf16), ((states, width), f32), ((1, width), f32)]
        + [((rows, model), f32), ((SEGS, width), f32), ((SEGS, width), f32), ((24, LANES), f32)]
    )
    return pl.pallas_call(
        mixer_back_kernel,
        out_shape=tuple(shaped(*dims, dtype=dtype) for dims, dtype in results),
        in_specs=[anywhere if k in streamed else WHOLE for k in range(25)],
        out_specs=(anywhere,) * len(results),
        scratch_shapes=[pltpu.VMEM(dims, dtype) for dims, dtype in kept]
        + chain_scratch(states, width)
        + [wide_scratch(rows, states)] * 4
        + [wide_scratch(rows, states, 1), wide_scratch(rows, states)]
        + [pltpu.VMEM((rows, LANES), f32)] * 2
        + [pltpu.SemaphoreType.DMA((10 + 2 * held,)), pltpu.SemaphoreType.DMA((len(results),)), pltpu.SemaphoreType.DMA((2,))]
        + relay_scratch(),
        compiler_params=roomy(62, collective_id=1, has_side_effects=True),
        cost_estimate=busy(rows * states * width),
        name="mixer_back",
    )(
        back, slots, probs, chosen, normed, router, middle, up, out_weight, gate, mixed, conv, step, raw, selection, pre, padded, entry,
        decay_log, step_weight, select, taps, packed, in_weight, tokens,
    )


def segmented(block):
    rows = block.shape[0]
    return block.reshape(SEGS, rows // SEGS, -1).transpose(1, 0, 2).reshape(rows, -1)


def in_order(block):
    rows = block.shape[0]
    return block.reshape(rows // SEGS, SEGS, -1).transpose(1, 0, 2).reshape(rows, -1)


def rms_scale(stream):
    return lax.rsqrt(jnp.mean(stream * stream, axis=-1, keepdims=True) + 1e-05)


def rms_back(stream, scale, gain, grad):
    grown = grad * gain
    along = jnp.mean(stream * grown, axis=-1, keepdims=True)
    return scale * grown - stream * (scale * scale * scale * along), jnp.sum(grad * stream * scale, axis=0)


def silu_slope(value):
    gate = jax.nn.sigmoid(value)
    return gate * (1.0 + value * (1.0 - gate))


def product(left, right):
    return jnp.dot(left, right, preferred_element_type=jnp.float32)


def across(left, right):
    return jnp.einsum("tk,dk->td", left, right, preferred_element_type=jnp.float32)


def summed_rows(left, right):
    return jnp.einsum("tk,td->kd", left, right, preferred_element_type=jnp.float32)


CHUNK = 1024
GELU_OUT = math.sqrt(2.0 / math.pi)
GELU_IN = 0.044715


def transposed_dot(left, right):
    return lax.dot_general(left, right, (((1,), (1,)), ((), ())), preferred_element_type=jnp.float32)


def column_dot(left, right):
    return lax.dot_general(left, right, (((0,), (0,)), ((), ())), preferred_element_type=jnp.float32)


def three_parts(value):
    parts, left = [], value
    for unused in range(3):
        part = left.astype(jnp.bfloat16)
        left = left - part.astype(jnp.float32)
        parts.append(part)
    return parts


def expert_pull_kernel(up_ref, second_ref, pull_ref):
    pull_ref[...] = transposed_dot(up_ref[...], second_ref[...]).astype(jnp.bfloat16)


def expert_pull(upstream, second):
    rows, width = upstream.shape
    hidden = second.shape[0]
    return pl.pallas_call(
        expert_pull_kernel,
        grid=(hidden // CHUNK,),
        out_shape=shaped(rows, hidden, dtype=jnp.bfloat16),
        in_specs=[pl.BlockSpec((rows, width), lambda i: (0, 0)), pl.BlockSpec((CHUNK, width), lambda i: (i, 0))],
        out_specs=pl.BlockSpec((rows, CHUNK), lambda i: (0, i)),
        compiler_params=roomy(60),
        cost_estimate=pl.CostEstimate(flops=2 * rows * hidden * width, bytes_accessed=2 * (width + rows) * hidden, transcendentals=0),
        name="expert_pull",
    )(upstream, second)


def expert_kernel(got_ref, up_ref, pull_ref, first_ref, second_ref, active_ref, grad_ref, value_ref, sent_ref, value, sent):
    step, last = pl.program_id(0), pl.num_programs(0) - 1
    width = up_ref.shape[1]
    first = first_ref[...]
    pre = jnp.dot(got_ref[:, :width], first, preferred_element_type=jnp.float32)
    square = pre * pre
    bent = jnp.tanh(pre * (GELU_OUT + GELU_OUT * GELU_IN * square))
    share = 0.5 + 0.5 * bent
    active = (pre * share).astype(jnp.bfloat16)
    slope = share + pre * (0.5 - 0.5 * bent * bent) * (GELU_OUT + 3.0 * GELU_OUT * GELU_IN * square)
    grad = (slope * pull_ref[...].astype(jnp.float32)).astype(jnp.bfloat16)
    active_ref[...] = active
    grad_ref[...] = grad
    more_value = jnp.dot(active, second_ref[...], preferred_element_type=jnp.float32)
    more_sent = transposed_dot(grad, first)

    @pl.when(step == 0)
    def begin():
        value[...] = more_value
        sent[...] = more_sent

    @pl.when(step > 0)
    def go_on():
        value[...] += more_value
        sent[...] += more_sent

    @pl.when(step == last)
    def finish():
        low = value[...].astype(jnp.bfloat16)
        value_ref[...] = low
        sent_ref[:, :width] = sent[...].astype(jnp.bfloat16)
        along = jnp.sum(low.astype(jnp.float32) * up_ref[...].astype(jnp.float32), axis=1, keepdims=True)
        place = lax.broadcasted_iota(jnp.int32, (sent_ref.shape[0], LANES), 1)
        tail = jnp.zeros(place.shape, jnp.float32)
        for k, part in enumerate(three_parts(along)):
            tail = jnp.where(place == k, part.astype(jnp.float32), tail)
        sent_ref[:, width:] = tail.astype(jnp.bfloat16)


def expert_layer(received, upstream, pull, first, second):
    rows, width = upstream.shape
    hidden = second.shape[0]
    wide = received.shape[1]

    def fixed(cols):
        return pl.BlockSpec((rows, cols), lambda i: (0, 0))

    chunk = pl.BlockSpec((rows, CHUNK), lambda i: (0, i))
    return pl.pallas_call(
        expert_kernel,
        grid=(hidden // CHUNK,),
        out_shape=(
            shaped(rows, hidden, dtype=jnp.bfloat16),
            shaped(rows, hidden, dtype=jnp.bfloat16),
            shaped(rows, width, dtype=jnp.bfloat16),
            shaped(rows, wide, dtype=jnp.bfloat16),
        ),
        in_specs=[
            fixed(wide),
            fixed(width),
            chunk,
            pl.BlockSpec((width, CHUNK), lambda i: (0, i)),
            pl.BlockSpec((CHUNK, width), lambda i: (i, 0)),
        ],
        out_specs=(chunk, chunk, fixed(width), fixed(wide)),
        scratch_shapes=[pltpu.VMEM((rows, width), jnp.float32)] * 2,
        compiler_params=roomy(60),
        cost_estimate=pl.CostEstimate(flops=6 * rows * hidden * width, bytes_accessed=4 * hidden * (width + rows), transcendentals=rows * hidden),
        name="expert_layer",
    )(received, upstream, pull, first, second)


def expert_sums_kernel(hidden_ref, received_ref, active_ref, up_ref, out_ref, scaled_received, scaled_up):
    pair = out_ref.shape[0]
    half = out_ref.shape[2]
    width = up_ref.shape[1]

    @pl.when(pl.program_id(0) == 0)
    def scale():
        parts = received_ref[:, width:].astype(jnp.float32)
        gate = parts[:, 0:1] + parts[:, 1:2] + parts[:, 2:3]
        scaled_received[...] = (received_ref[:, :width].astype(jnp.float32) * gate).astype(jnp.bfloat16)
        scaled_up[...] = (up_ref[...].astype(jnp.float32) * gate).astype(jnp.bfloat16)

    for which, (left_ref, right_ref) in enumerate(((hidden_ref, scaled_received), (active_ref, scaled_up))):
        total = column_dot(left_ref[...], right_ref[...]).astype(jnp.bfloat16)
        for i in range(pair):
            out_ref[i, which] = total[i * half : (i + 1) * half]


def expert_sums(grad_hidden, received, activated, upstream, owners):
    rows, hidden = grad_hidden.shape
    width = upstream.shape[1]
    pair = 2
    chunk = pl.BlockSpec((rows, pair * hidden // owners), lambda i: (0, i))

    def fixed(cols):
        return pl.BlockSpec((rows, cols), lambda i: (0, 0))

    return pl.pallas_call(
        expert_sums_kernel,
        grid=(owners // pair,),
        out_shape=shaped(owners, 2, hidden // owners, width, dtype=jnp.bfloat16),
        in_specs=[chunk, fixed(received.shape[1]), chunk, fixed(width)],
        out_specs=pl.BlockSpec((pair, 2, hidden // owners, width), lambda i: (i, 0, 0, 0)),
        scratch_shapes=[pltpu.VMEM((rows, width), jnp.bfloat16)] * 2,
        compiler_params=roomy(60),
        cost_estimate=pl.CostEstimate(flops=4 * rows * hidden * width, bytes_accessed=4 * hidden * (width + rows), transcendentals=0),
        name="expert_sums",
    )(grad_hidden, received, activated, upstream)


ORDERS = ("xyz", "yzx", "zxy")
PIECE = 16


def shares_kernel(
    conv_cols, gate_cols, token_ref, out_cols, middle_ref, left_ref, right_ref, narrow_ref, sum_ref, in_ref, out_ref, made, taken,
    half_a, half_b, half_c, one_a, one_b, one_c, sends, arrivals):
    seq, expert = lax.axis_index("seq"), lax.axis_index("expert")
    core = lax.rem(expert, 2)
    place = {"y": lax.div(seq, 4), "z": lax.rem(seq, 4), "x": lax.div(expert, 2)}
    third = token_ref.shape[1] // len(ORDERS)
    streams = [(L, q) for L in range(len(ORDERS)) for q in range(4)]

    def flip(i):
        return i + 1 - 2 * lax.rem(i, 2)

    def device(**moved):
        at = dict(place, **moved)
        return {"seq": at["y"] * 4 + at["z"], "expert": at["x"] * 2 + at.get("core", core)}

    partners = [device(core=1 - core)]
    for axis in "xyz":
        partners += [device(**{axis: flip(place[axis])}), device(**{axis: 3 - place[axis]})]
    barrier = pltpu.get_barrier_semaphore()
    for partner in partners:
        pl.semaphore_signal(barrier, inc=1, device_id=partner, device_id_type=pl.DeviceIdType.MESH)
    pl.semaphore_wait(barrier, len(partners))

    def send(source, target, partner, stream, number):
        k = streams.index(stream)
        copy = pltpu.make_async_remote_copy(
            src_ref=source, dst_ref=target, send_sem=sends.at[k, number], recv_sem=arrivals.at[k, number],
            device_id=partner, device_id_type=pl.DeviceIdType.MESH,
        )
        copy.start()
        return copy

    def add(target, source, unit):
        def step(i, unused):
            target[i] = target[i] + source[i]
            return unused

        lax.fori_loop(0, unit, step, 0, unroll=min(unit, 8))

    inner = out_cols.shape[1]
    for source, target, base in ((conv_cols, in_ref, 0), (gate_cols, in_ref, inner), (out_cols, out_ref, 0)):

        def turn_over(k, unused, source=source, target=target, base=base):
            spot = pl.ds(pl.multiple_of(k * LANES, LANES), LANES)
            target[pl.ds(pl.multiple_of(base + k * LANES, LANES), LANES), :] = source[:, spot].T
            return unused

        lax.fori_loop(0, source.shape[1] // LANES, turn_over, 0)

    pending = {}
    for L, order in enumerate(ORDERS):
        lanes = pl.ds(L * third, third)
        narrow = narrow_ref[:, lanes].astype(jnp.bfloat16)

        def block(s, unused):
            y, z = lax.div(s, 4), lax.rem(s, 4)
            by_in = jnp.dot(
                in_ref[pl.ds(pl.multiple_of(s * 288, 16), 288), :], token_ref[:, lanes], preferred_element_type=jnp.float32
            ).astype(jnp.bfloat16)
            here = pl.ds(pl.multiple_of(s * 144, 16), 144)
            by_out = jnp.dot(out_ref[here, :], middle_ref[:, lanes], preferred_element_type=jnp.float32)
            left, right = left_ref[here, :], right_ref[here, :]
            for x in range(4):
                at = {"x": x, "y": y, "z": z}
                slot = (at[order[0]] * 4 + at[order[1]]) * 4 + at[order[2]]
                rows = by_in[72 * x : 72 * x + 72]
                more = by_out[36 * x : 36 * x + 36].astype(jnp.bfloat16)
                for q in range(4):
                    made[L, q, slot] = rows[16 * q : 16 * q + 16]
                made[L, 4, slot, 0:8] = rows[64:]
                made[L, 4, slot, 8:16] = more[:8]
                made[L, 5, slot] = more[8:24]
                made[L, 6, slot, 0:12] = more[24:]
                made[L, 6, slot, 12:16] = narrow[8:12]
                made[L, 7, slot, 8:16] = narrow[0:8]
                last = jnp.concatenate([left[36 * x : 36 * x + 36], right[36 * x : 36 * x + 36]], axis=0)
                for part in range(third // LANES):
                    k = 8 * (L * (third // LANES) + part)
                    made[L, 7, slot, 0:8, part * LANES : (part + 1) * LANES] = last[k : k + 8].astype(jnp.bfloat16)
            return unused

        lax.fori_loop(0, 16, block, 0, unroll=2)
        for q in range(4):
            pending[L, q] = [
                send(made.at[L, 4 * (1 - core) + q], taken.at[L, q], device(core=1 - core), (L, q), 0)
            ]

    halves, ones = (half_a, half_b, half_c), (one_a, one_b, one_c)
    holding = {}
    for L, q in streams:
        for copy in pending[L, q]:
            copy.wait()
        add(taken.at[L, q], made.at[L, 4 * core + q], 64)
        holding[L, q] = taken.at[L, q]
        pending[L, q] = start_halves(L, q, 0, holding[L, q], halves, place, flip, device, send)
    for turn in range(3):
        unit = 16 >> (2 * turn)
        for L, q in streams:
            axis = ORDERS[L][turn]
            i = place[axis]
            for copy in pending[L, q]:
                copy.wait()
            other = 3 - i if q < 2 else flip(i)
            got = halves[turn].at[L, q]
            add(got.at[0], holding[L, q].at[pl.ds(i * unit, unit)], unit)
            add(got.at[1], holding[L, q].at[pl.ds(other * unit, unit)], unit)
            partner = device(**{axis: other})
            pending[L, q] = [send(got.at[1], ones[turn].at[L, q], partner, (L, q), 3 + 3 * turn)]
        for L, q in streams:
            for copy in pending[L, q]:
                copy.wait()
            got = ones[turn].at[L, q]
            if turn < 2:
                add(got, halves[turn].at[L, q, 0], unit)
                holding[L, q] = got
                pending[L, q] = start_halves(L, q, turn + 1, got, halves, place, flip, device, send)
            else:
                whole = got[0].astype(jnp.float32) + halves[turn][L, q, 0, 0].astype(jnp.float32)
                sum_ref[4 * core + q, :, L * third : (L + 1) * third] = whole
    here = sum_ref.at[pl.ds(4 * core, 4)]
    send(here, here, device(core=1 - core), (0, 0), 10).wait()


def start_halves(L, q, turn, source, halves, place, flip, device, send):
    axis = ORDERS[L][turn]
    unit = 16 >> (2 * turn)
    i = place[axis]
    partner = flip(i) if q < 2 else 3 - i
    second = 3 - partner if q < 2 else flip(partner)
    target = halves[turn].at[L, q]
    return [
        send(source.at[pl.ds(partner * unit, unit)], target.at[0], device(**{axis: partner}), (L, q), 1 + 3 * turn),
        send(source.at[pl.ds(second * unit, unit)], target.at[1], device(**{axis: partner}), (L, q), 2 + 3 * turn),
    ]


def shares(conv_cols, gate_cols, tokens, out_cols, middle, left, right, narrow):
    width = tokens.shape[1]
    rows, inner = out_cols.shape
    third = width // len(ORDERS)

    def slots(*lead):
        return pltpu.VMEM((len(ORDERS),) + lead + (PIECE, third), jnp.bfloat16)

    return pl.pallas_call(
        shares_kernel,
        out_shape=shaped(8, PIECE, width),
        in_specs=[WHOLE] * 8,
        out_specs=WHOLE,
        scratch_shapes=[pltpu.VMEM((2 * inner, rows), jnp.bfloat16), pltpu.VMEM((inner, rows), jnp.bfloat16)]
        + [slots(8, 64), slots(4, 64)]
        + [slots(4, 2, 16 >> (2 * turn)) for turn in range(3)]
        + [slots(4, 16 >> (2 * turn)) for turn in range(3)]
        + [pltpu.SemaphoreType.DMA((12, 11))] * 2,
        compiler_params=roomy(60, collective_id=2, has_side_effects=True),
        name="shares",
    )(conv_cols, gate_cols, tokens, out_cols, middle, left, right, narrow)


def local(
    tokens,
    expert_index,
    cotangent,
    first_gain,
    in_weight,
    conv_weight,
    conv_bias,
    select_weight,
    step_weight,
    step_bias,
    decay_log,
    skip_gain,
    out_weight,
    second_gain,
    router_weight,
    expert_first,
    expert_second,
):
    bf16, f32 = jnp.bfloat16, jnp.float32
    stream = segmented(tokens[0])
    routes = segmented(expert_index[0])[:, 0]
    upstream = segmented(cotangent[0])
    row_count, model_width = stream.shape
    seat_count = 2 * row_count
    inner = conv_bias.shape[0]
    rank = step_weight.shape[0]
    states = decay_log.shape[0]
    taps = conv_weight.shape[0]
    expert_count = router_weight.shape[1]
    capacity = 2 * row_count // expert_count
    seqs, experts = lax.axis_size("seq"), lax.axis_size("expert")
    reach = (taps - 1) * SEGS

    picks = (routes[:, None] == jnp.arange(expert_count, dtype=jnp.int32)[None, :]).astype(bf16)
    earlier = jnp.arange(row_count)[:, None] > jnp.arange(row_count)[None, :]
    ahead = product(earlier.astype(bf16), picks)
    chosen = picks.astype(f32)
    slot_index = routes * capacity + jnp.sum(ahead * chosen, axis=1).astype(jnp.int32)
    seats = jnp.arange(expert_count * capacity, dtype=jnp.int32)
    placing = (seats[:, None] == slot_index[None, :]).astype(bf16)

    def seated(rows):
        return product(placing, rows).astype(bf16)

    def swapped(rows):
        parts = rows.reshape(expert_count, capacity, -1)
        parts = lax.all_to_all(parts, "expert", split_axis=0, concat_axis=0, tiled=True)
        return parts.reshape(expert_count * capacity, -1)

    def unseated(rows):
        return jnp.einsum("st,sd->td", placing, rows, preferred_element_type=f32)

    upstream_there = swapped(seated(upstream))

    packed = jnp.concatenate([conv_bias, step_bias, skip_gain, first_gain, second_gain]).reshape(4, inner)
    slot_column = slot_index[:, None]
    (
        normed_in, gate_input, padded, preact, conv_out, step_raw, step_size, selection, first, mixer_out, gated,
        middle, normed_mid, router_probs, gate_wide, leaving,
    ) = mixer(
        stream, packed, in_weight, conv_weight, select_weight, step_weight, decay_log, out_weight, router_weight, slot_column, seat_count
    )
    leaving, upstream_there = lax.optimization_barrier((leaving, upstream_there))
    received = swapped(leaving)
    pull = expert_pull(upstream_there, expert_second[0])
    activated, grad_hidden, value_there, grad_there = expert_layer(
        received, upstream_there, pull, expert_first[0], expert_second[0]
    )
    back = swapped(grad_there)
    expert_grads = expert_sums(grad_hidden, received, activated, upstream_there, seqs)
    expert_grads, value_there, back = lax.optimization_barrier((expert_grads, value_there, back))
    value_home = swapped(value_there)
    expert_share = lax.psum_scatter(
        expert_grads.reshape(-1, model_width), "seq", scatter_dimension=0, tiled=True
    ).reshape(2, -1, model_width)
    middle_low, grad_gate_input, grad_conv_input, left, right, narrow, grad_tokens = mixer_back(
        back, slot_column, router_probs, gate_wide, normed_mid, router_weight, middle, upstream, out_weight, gate_input, mixer_out, conv_out,
        step_size, step_raw, selection, preact, padded, first, decay_log, step_weight, select_weight, conv_weight, packed, in_weight, stream,
    )
    middle_low, value_home = lax.optimization_barrier((middle_low, value_home))
    mixed = middle + gate_wide[:, 0:1] * unseated(value_home)

    devices = seqs * experts
    each, fewer = inner // devices, model_width // devices
    grad_conv_input, expert_share = lax.optimization_barrier((grad_conv_input, expert_share))
    sums = shares(grad_conv_input, grad_gate_input, normed_in, gated, middle_low, left, right, narrow)
    sums = sums.reshape(-1, model_width)
    core = lax.axis_index("expert") % 2
    in_share = lax.dynamic_slice_in_dim(sums, 2 * each * core, 2 * each)
    out_share = lax.dynamic_slice_in_dim(sums, 4 * each + each * core, each)
    small = sums[112:120].reshape(8, -1, LANES).transpose(1, 0, 2).reshape(2, 2 * each, LANES)
    small = lax.dynamic_slice_in_dim(small, each * core, each, axis=1)
    rows_sum = small[0, :, rank + 2 * states :]
    owner = lax.axis_index("seq") * experts + lax.axis_index("expert")
    narrow_sum = jnp.concatenate([sums[120:128], sums[108:110]])
    narrow_sum = lax.dynamic_slice_in_dim(narrow_sum, owner * fewer, fewer, axis=1)
    return (
        in_order(mixed.astype(bf16))[None],
        in_order(grad_tokens)[None],
        narrow_sum[0],
        in_share.T,
        rows_sum[:, states : states + taps].T,
        rows_sum[:, states + taps],
        small[0, :, : rank + 2 * states],
        small[1, :, :rank].T,
        rows_sum[:, states + taps + 1],
        rows_sum[:, :states].T,
        rows_sum[:, states + taps + 2],
        out_share,
        narrow_sum[1],
        narrow_sum[2:].T,
        expert_share[0].T.astype(f32)[None],
        expert_share[1].astype(f32)[None],
    )


def solution(mesh):
    return jax.shard_map(
        local,
        mesh=mesh,
        in_specs=(
            P("expert", "seq", None),
            P("expert", "seq", None),
            P("expert", "seq", None),
            P(),
            P(),
            P(),
            P(),
            P(),
            P(),
            P(),
            P(),
            P(),
            P(),
            P(),
            P(),
            P("expert", None, None),
            P("expert", None, None),
        ),
        out_specs=(
            P("expert", "seq", None),
            P("expert", "seq", None),
            P(("seq", "expert")),
            P(None, ("seq", "expert")),
            P(None, ("seq", "expert")),
            P(("seq", "expert")),
            P(("seq", "expert"), None),
            P(None, ("seq", "expert")),
            P(("seq", "expert")),
            P(None, ("seq", "expert")),
            P(("seq", "expert")),
            P(("seq", "expert"), None),
            P(("seq", "expert")),
            P(("seq", "expert"), None),
            P("expert", None, "seq"),
            P("expert", "seq", None),
        ),
        check_vma=False,
    )
```

profile of v0, /device:TPU:1, one launch (start us, length us, event | category | flops | bytes accessed | tf_op | source)
XLA Modules:
  0.0 337.4 jit_solution(17251803473921561863)
XLA Ops:
  7.7 1.3 reduce.11
  9.5 2.6 convolution_convert_fusion
  12.1 5.9 %all-to-all-start = ((bf16[8,64,1152]{2,1,0:T(8,128)(2,1)}), bf16[8,64,1152]{2,1,0:T(8,128)(2,1)S(1)}, u32[]{:S(2)}, u32[]{:S(2)}) async-start(bf16[8,64,1152]{2,1,0:T(8,128)(2,1)} %bitcast.8), calls=%async_computation | async-start | bytes 2359296 | tf_op jit(solution)/shard_map/all_to_all | solution.py:1187
  19.1 1.0 copy.86
  20.1 1.1 copy.71.select_ref
  22.7 50.0 %mixer.1 = (bf16[256,1152]{1,0:T(8,128)(2,1)}, f32[256,2304]{1,0:T(8,128)}, f32[280,2304]{1,0:T(8,128)}, f32[256,2304]{1,0:T(8,128)}, f32[256,2304]{1,0:T(8,128)...) custom-call(bf16[256,1152]{1,0:T(8,128)(2,1)} %bitcast.96, ...), custom_call_target="tpu_custom_call" | custom-call | flops 38654705664 | bytes 150994944 | tf_op jit(solution)/shard_map/mixer/pallas_call | solution.py:712
  72.7 1.0 copy-done.5
  73.7 7.9 %all-to-all-start.1 = ((bf16[8,64,1280]{2,1,0:T(8,128)(2,1)}), bf16[8,64,1280]{2,1,0:T(8,128)(2,1)S(1)}, u32[]{:S(2)}, u32[]{:S(2)}) async-start(bf16[8,64,1280]{2,1,0:T(8,128)(2,1)} %bitcast.84), calls=%async_computation.1 | async-start | bytes 2621440 | tf_op jit(solution)/shard_map/all_to_all | solution.py:1187
  81.7 8.1 %expert_pull.1.pull_ref = bf16[512,3072]{1,0:T(8,128)(2,1)} custom-call(bf16[512,1152]{1,0:T(8,128)(2,1)} %bitcast.90, bf16[3072,1152]{1,0:T(8,128)(2,1)} %bitcast.102), custom_call_target="tpu_custom_call" | custom-call | flops 3623878656 | bytes 10223616 | tf_op jit(solution)/shard_map/expert_pull/pallas_call | solution.py:852
  89.8 9.8 %all-to-all-done.1 = bf16[8,64,1280]{2,1,0:T(8,128)(2,1)S(1)} async-done(((bf16[8,64,1280]{2,1,0:T(8,128)(2,1)}), bf16[8,64,1280]{2,1,0:T(8,128)(2,1)S(1)}, u32[]{:S(2)}, u32[]{:S(2)}) %all-to-all-start.1) | async-done | bytes 1310752 | tf_op jit(solution)/shard_map/all_to_all | solution.py:1187
  99.6 1.0 copy-done.3
  100.6 21.8 %expert_layer.1 = (bf16[512,3072]{1,0:T(8,128)(2,1)}, bf16[512,3072]{1,0:T(8,128)(2,1)}, bf16[512,1152]{1,0:T(8,128)(2,1)}, bf16[512,1280]{1,0:T(8,128)(2,1)}) custom-call(bf16[512,1280]{1,0:T(8,128)(2,1)} %bitcast.85, bf16[512,1152]{1,0:T(8,128)(2,1)} %bitcast.91, bf16[512,3072]{1,0:T(8,128)(2,1)} %expert_pull.1.pull_ref, bf16[1152,3072]{1,0:T(8,128)(2,1)} %bitcast.104, ...), custom_call_target="tpu_custom_call" | custom-call | flops 10871635968 | bytes 20447232 | tf_op jit(solution)/shard_map/expert_layer/pallas_call | solution.py:912
  122.5 4.4 %all-to-all-start.2 = ((bf16[8,64,1280]{2,1,0:T(8,128)(2,1)}), bf16[8,64,1280]{2,1,0:T(8,128)(2,1)S(1)}, u32[]{:S(2)}, u32[]{:S(2)}) async-start(bf16[8,64,1280]{2,1,0:T(8,128)(2,1)} %bitcast.87), calls=%async_computation.2 | async-start | bytes 2621440 | tf_op jit(solution)/shard_map/all_to_all | solution.py:1187
  126.8 15.2 %expert_sums.1 = bf16[16,2,192,1152]{3,2,1,0:T(8,128)(2,1)} custom-call(bf16[512,3072]{1,0:T(8,128)(2,1)} %get-tuple-element.57.hidden_ref, bf16[512,1280]{1,0:T(8,128)(2,1)} %bitcast.86, bf16[512,3072]{1,0:T(8,128)(2,1)} %get-tuple-element.58.active_ref, bf16[512,1152]{1,0:T(8,128)(2,1)} %bitcast.92), custom_call_target="tpu_custom_call" | custom-call | flops 7247757312 | bytes 20447232 | tf_op jit(solution)/shard_map/expert_sums/pallas_call | solution.py:963
  142.0 2.7 all-to-all-done.2
  144.8 1.1 copy-done.2
  145.8 1.0 copy-done
  146.9 1.0 copy.85
  148.0 4.3 %all-to-all-start.3 = ((bf16[8,64,1152]{2,1,0:T(8,128)(2,1)}), bf16[8,64,1152]{2,1,0:T(8,128)(2,1)S(1)}, u32[]{:S(2)}, u32[]{:S(2)}) async-start(bf16[8,64,1152]{2,1,0:T(8,128)(2,1)} %bitcast.88), calls=%async_computation.3 | async-start | bytes 2359296 | tf_op jit(solution)/shard_map/all_to_all | solution.py:1187
  152.3 81.2 %mixer_back.1 = (bf16[256,1152]{1,0:T(8,128)(2,1)}, bf16[256,2304]{1,0:T(8,128)(2,1)}, bf16[256,2304]{1,0:T(8,128)(2,1)}, f32[2304,128]{1,0:T(8,128)}, f32[2304,...) custom-call(bf16[512,1280]{1,0:T(8,128)(2,1)} %bitcast.83, s32[256,1]{1,0:T(8,128)} %copy.73.slot_ref, ...), custom_call_target="tpu_custom_call" | custom-call | flops 38654705664 | bytes 150994944 | tf_op jit(solution)/shard_map/mixer_back/pallas_call | solution.py:765
  233.6 2.6 copy.79
  237.7 8.7 %reduce-scatter.2.cloned.1.call-done = bf16[384,1152]{1,0:T(8,128)(2,1)} async-done(((bf16[6144,1152]{1,0:T(8,128)(2,1)}), bf16[384,1152]{1,0:T(8,128)(2,1)}) %reduce-scatter.2.cloned.1.call-update) | async-done | bytes 884752 | tf_op jit(solution)/shard_map/reduce_scatter | solution.py:1213
  246.3 75.3 %shares.1 = f32[8,16,1152]{2,1,0:T(8,128)} custom-call(bf16[256,2304]{1,0:T(8,128)(2,1)} %get-tuple-element.79.conv_cols, bf16[256,2304]{1,0:T(8,128)(2,1)} %get-tuple-element.80.gate_cols, bf16[256,1152]{1,0:T(8,128)(2,1)} %get-tuple-element.81.token_ref, bf16[256,2304]{1,0:T(8,128)(2,1)} %get-tuple-element.82.out_cols, ...), custom_call_target="tpu_custom_call" | custom-call | tf_op jit(solution)/shard_map/shares/pallas_call | solution.py:1125
  325.9 1.3 slice_convert_fusion
  (70 shorter events, 12.6 us)
Async XLA Ops:
  12.1 6.9 %copy-start.7 = (bf16[1,256,1152]{2,1,0:T(8,128)(2,1)S(1)}, bf16[1,256,1152]{2,1,0:T(8,128)(2,1)}, u32[]{:S(2)}) copy-start(bf16[1,256,1152]{2,1,0:T(8,128)(2,1)} %param.17) | copy-start | bytes 1769476
  12.1 60.6 %all-to-all-start = ((bf16[8,64,1152]{2,1,0:T(8,128)(2,1)}), bf16[8,64,1152]{2,1,0:T(8,128)(2,1)S(1)}, u32[]{:S(2)}, u32[]{:S(2)}) async-start(bf16[8,64,1152]{2,1,0:T(8,128)(2,1)} %bitcast.8), calls=%async_computation | async-start | bytes 2359296 | tf_op jit(solution)/shard_map/all_to_all | solution.py:1187
  18.1 2.0 copy-start.8
  18.2 2.9 copy-start.10
  19.0 3.0 copy-start.11
  19.0 3.0 copy-start.12
  19.0 3.0 copy-start.13
  19.0 3.0 copy-start.14
  19.0 3.0 copy-start.15
  72.7 1.0 copy-start.5
  73.7 25.9 %all-to-all-start.1 = ((bf16[8,64,1280]{2,1,0:T(8,128)(2,1)}), bf16[8,64,1280]{2,1,0:T(8,128)(2,1)S(1)}, u32[]{:S(2)}, u32[]{:S(2)}) async-start(bf16[8,64,1280]{2,1,0:T(8,128)(2,1)} %bitcast.84), calls=%async_computation.1 | async-start | bytes 2621440 | tf_op jit(solution)/shard_map/all_to_all | solution.py:1187
  99.6 1.0 copy-start.3
  122.5 22.3 %all-to-all-start.2 = ((bf16[8,64,1280]{2,1,0:T(8,128)(2,1)}), bf16[8,64,1280]{2,1,0:T(8,128)(2,1)S(1)}, u32[]{:S(2)}, u32[]{:S(2)}) async-start(bf16[8,64,1280]{2,1,0:T(8,128)(2,1)} %bitcast.87), calls=%async_computation.2 | async-start | bytes 2621440 | tf_op jit(solution)/shard_map/all_to_all | solution.py:1187
  126.8 119.5 %reduce-scatter.2.cloned.1.call-start = ((), (), s32[]{:S(2)}) async-start(), calls=%async_computation.5 | async-start | bytes 15040512 | tf_op jit(solution)/shard_map/reduce_scatter | solution.py:1213
  144.8 1.1 copy-start.2
  145.8 1.1 copy-start
  146.9 1.0 copy-start.9
  148.0 88.2 %all-to-all-start.3 = ((bf16[8,64,1152]{2,1,0:T(8,128)(2,1)}), bf16[8,64,1152]{2,1,0:T(8,128)(2,1)S(1)}, u32[]{:S(2)}, u32[]{:S(2)}) async-start(bf16[8,64,1152]{2,1,0:T(8,128)(2,1)} %bitcast.88), calls=%async_computation.3 | async-start | bytes 2359296 | tf_op jit(solution)/shard_map/all_to_all | solution.py:1187
  233.6 2.7 copy-start.4
  246.3 79.6 %copy-start.6 = (bf16[384,1152]{1,0:T(8,128)(2,1)S(1)}, bf16[384,1152]{1,0:T(8,128)(2,1)}, u32[]{:S(2)}) copy-start(bf16[384,1152]{1,0:T(8,128)(2,1)} %reduce-scatter.2.cloned.1.call-done) | copy-start | bytes 2654212
  325.9 3.3 copy-start.1
Sparse Core Ops, SparseCore 0:
  146.0 100.3 reduce-scatter.1
where the time goes:
time: 338 us; the launch traced here: 337 us
  Pallas kernels  252 us (75%)
  starting transfers between devices  22.6 us (7%)
  local copies, waits for them, and re-layouts  21.5 us (6%)
  waiting for transfers between devices  21.2 us (6%)
  between operations  14.3 us (4%)
  matrix products  3.4 us (1%)
    pallas_call x1, Pallas kernels, mixer_back(): pl.pallas_call(mixer_back_kernel, out_shape=tuple((shaped(*dims, dtype=dt...  81.2 us
    pallas_call x1, Pallas kernels, shares(): pl.pallas_call(shares_kernel, out_shape=shaped(8, PIECE, width), in_specs...  75.3 us
    pallas_call x1, Pallas kernels, mixer(): pl.pallas_call(mixer_kernel, out_shape=tuple((shaped(*dims, dtype=dtype)...  50 us
    all_to_all x4, starting transfers between devices, swapped(): lax.all_to_all(parts, 'expert', split_axis=0, concat_axis=0, tiled=True)  22.6 us
    pallas_call x1, Pallas kernels, expert_layer(): pl.pallas_call(expert_kernel, grid=(hidden // CHUNK,), out_shape=(shaped(...  21.8 us
    pallas_call x1, Pallas kernels, expert_sums(): pl.pallas_call(expert_sums_kernel, grid=(owners // pair,), out_shape=shap...  15.2 us
    all_to_all x4, waiting for transfers between devices, swapped(): lax.all_to_all(parts, 'expert', split_axis=0, concat_axis=0, tiled=True)  12.5 us
    reduce_scatter x1, waiting for transfers between devices, local(): lax.psum_scatter(expert_grads.reshape(-1, model_width), 'seq', scatter_di...  8.65 us
  transfers between devices with their start and end apart: 5, of which 3 were waited for; matrix products, arithmetic and copies ran while one was open for 3% of the time, Pallas kernels for 46%

commit v1 on v0

--- a/solution.py
+++ b/solution.py
@@ -202,8 +202,32 @@
     lax.fori_loop(0, blocks, block, 0)
 
 
+def expert_peers():
+    me = lax.axis_index("expert")
+    return [lax.rem(me + k, EXPERTS) for k in range(1, EXPERTS)]
+
+
+def seats_of(device):
+    return pl.ds(pl.multiple_of(device * CAPACITY, CAPACITY), CAPACITY)
+
+
+def trade(source, target, send_sems, recv_sems):
+    me = lax.axis_index("expert")
+    copies = [
+        pltpu.make_async_remote_copy(
+            src_ref=source.at[seats_of(peer)], dst_ref=target.at[seats_of(me)], send_sem=send_sems.at[k], recv_sem=recv_sems.at[k],
+            device_id={"expert": peer}, device_id_type=pl.DeviceIdType.MESH,
+        )
+        for k, peer in enumerate(expert_peers())
+    ]
+    copies.append(pltpu.make_async_copy(source.at[seats_of(me)], target.at[seats_of(me)], send_sems.at[EXPERTS - 1]))
+    for copy in copies:
+        copy.start()
+    return copies
+
+
 class Relay:
-    def __init__(self, later, log_ref, log_rows, in_ref, message, got, row, rows_got, above, made, sends, arrivals, chained=False):
+    def __init__(self, later, log_ref, log_rows, in_ref, message, got, row, rows_got, above, made, sends, arrivals, others=()):
         self.later, self.log_rows, self.message, self.got = later, log_rows, message, got
         self.row, self.rows_got, self.above, self.made, self.in_ref = row, rows_got, above, made, in_ref
         self.sends, self.arrivals = sends, arrivals
@@ -219,8 +243,7 @@
         self.flying = {}
         barrier = pltpu.get_barrier_semaphore()
         peers = [self.across(k) for k in range(1, GRID)] + [self.along(k) for k in range(1, GRID)]
-        if chained:
-            peers += [self.onward(1), self.onward(-1)]
+        peers += [self.onward(1), self.onward(-1)] + list(others)
         for peer in peers:
             pl.semaphore_signal(barrier, inc=1, device_id=peer, device_id_type=pl.DeviceIdType.MESH)
         self.peers = len(peers)
@@ -320,22 +343,30 @@
     scan(2)
 
 
-def named_experts(slot_ref, rows):
-    slot = slot_ref[...]
-    first = lax.broadcasted_iota(jnp.int32, (rows, EXPERTS), 1) * CAPACITY
-    return jnp.where((slot >= first) & (slot < first + CAPACITY), 1.0, 0.0)
-
-
-def seated_rows(slot_ref, rows, seats):
-    return jnp.where(lax.broadcasted_iota(jnp.int32, (rows, seats), 1) == slot_ref[...], 1.0, 0.0).astype(jnp.bfloat16)
+def named_experts(slots, rows):
+    first = (lax.broadcasted_iota(jnp.int32, (rows, EXPERTS), 1) * CAPACITY).astype(jnp.float32)
+    return jnp.where((slots >= first) & (slots < first + CAPACITY), 1.0, 0.0)
+
+
+def seated_rows(slots, rows, seats):
+    seat = lax.broadcasted_iota(jnp.int32, (rows, seats), 1).astype(jnp.float32)
+    return jnp.where(seat == slots, 1.0, 0.0).astype(jnp.bfloat16)
+
+
+def slots_of(routes, rows):
+    expert = lax.broadcasted_iota(jnp.int32, (rows, EXPERTS), 1)
+    named = jnp.where(expert == routes, 1.0, 0.0)
+    later = lax.broadcasted_iota(jnp.int32, (rows, rows), 0) > lax.broadcasted_iota(jnp.int32, (rows, rows), 1)
+    ahead = jnp.dot(jnp.where(later, 1.0, 0.0).astype(jnp.bfloat16), named.astype(jnp.bfloat16), preferred_element_type=jnp.float32)
+    return jnp.sum(named * (ahead + (expert * CAPACITY).astype(jnp.float32)), axis=1, keepdims=True)
 
 
 def mixer_kernel(
-    token_ref, row_ref, in_hbm, tap_ref, select_ref, step_weight_ref, log_ref, out_hbm, router_ref, slot_ref,
+    token_ref, up_ref, row_ref, in_hbm, tap_ref, select_ref, step_weight_ref, log_ref, out_hbm, router_ref, route_ref,
     normed_out, gate_out, padded_out, pre_out, conv_out, raw_out, step_out, sel_out, entry_out, mixer_out, gated_out,
-    middle_out, normed_mid_out, probs_out, chosen_out, leaving_out,
-    normed, in_ref, out_ref, padded, gate, pre, conv, raw, step, sel, entry, mixer, gated, middle, normed_mid, probs, chosen, leaving,
-    tail, tail_got, part_ref, span_ref, wide_in, wide_out, loads, saves, passing, log_rows, relay_in, *relayed
+    middle_out, normed_mid_out, probs_out, chosen_out, leaving_out, slot_out, up_out,
+    normed, in_ref, out_ref, padded, gate, pre, conv, raw, step, sel, entry, mixer, gated, middle, normed_mid, probs, chosen, leaving, slots, up_seated,
+    tail, tail_got, part_ref, span_ref, wide_in, wide_out, loads, saves, passing, goes, comes, log_rows, relay_in, *relayed
 ):
     rows, width = step.shape
     model = token_ref.shape[1]
@@ -359,7 +390,7 @@
         copy.start()
         saving.append(copy)
 
-    relay = Relay(False, log_ref, log_rows, relay_in, *relayed, chained=True)
+    relay = Relay(False, log_ref, log_rows, relay_in, *relayed, others=[{"expert": peer} for peer in expert_peers()])
 
     stream = token_ref[...].astype(jnp.float32)
     normed[...] = (stream * rms_scale(stream) * gain_ref[...]).astype(jnp.bfloat16)
@@ -371,12 +402,18 @@
     for k in range(taps - 1):
         row = reach + rows - (taps - 1 - k) * SEGS + SEGS - 1
         tail[k : k + 1, :] = padded[row : row + 1, :]
+    slot = slots_of(route_ref[...], rows)
+    slots[...] = jnp.broadcast_to(slot, slots.shape)
+    save(slots, slot_out)
+    seating = seated_rows(slot, rows, leaving.shape[0])
+    up_seated[...] = column_dot(seating, up_ref[...]).astype(jnp.bfloat16)
     relay.meet()
     handing = pltpu.make_async_remote_copy(
         src_ref=tail, dst_ref=tail_got, send_sem=passing.at[0], recv_sem=passing.at[1],
         device_id=relay.onward(1), device_id_type=pl.DeviceIdType.MESH,
     )
     handing.start()
+    trading = trade(up_seated, up_out, goes, comes)
     for k in range(pieces // 2, pieces):
         loading[k].wait()
         spot = slice((k - pieces // 2) * cut, (k - pieces // 2 + 1) * cut)
@@ -452,30 +489,30 @@
     grown = jnp.exp(logits - jnp.max(logits, axis=1, keepdims=True))
     probs[...] = grown / jnp.sum(grown, axis=1, keepdims=True)
     save(probs, probs_out)
-    gate_value = jnp.sum(named_experts(slot_ref, rows) * probs[...], axis=1, keepdims=True)
+    gate_value = jnp.sum(named_experts(slots[:, 0:1], rows) * probs[...], axis=1, keepdims=True)
     chosen[...] = jnp.broadcast_to(gate_value, (rows, LANES))
     save(chosen, chosen_out)
     place = lax.broadcasted_iota(jnp.int32, (rows, LANES), 1)
     parts = jnp.zeros((rows, LANES), jnp.float32)
     for k, piece in enumerate(three_parts(gate_value)):
         parts = jnp.where(place == k, piece.astype(jnp.float32), parts)
-    seating = seated_rows(slot_ref, rows, leaving.shape[0])
+    seating = seated_rows(slots[:, 0:1], rows, leaving.shape[0])
     leaving[:, :model] = column_dot(seating, normed_mid[...]).astype(jnp.bfloat16)
     leaving[:, model:] = column_dot(seating, parts.astype(jnp.bfloat16)).astype(jnp.bfloat16)
     save(leaving, leaving_out)
-    for copy in saving:
+    for copy in saving + trading:
         copy.wait()
 
 
 def mixer_back_kernel(
     back_hbm, slot_ref, probs_ref, chosen_ref, normed_ref, router_ref, middle_ref, up_ref, out_hbm, gate_hbm,
     mixer_hbm, conv_hbm, step_hbm, raw_hbm, sel_ref, pre_hbm, padded_hbm, entry_hbm, log_ref, step_weight_ref, select_ref,
-    tap_ref, packed_ref, in_hbm, token_ref,
-    low_out, gate_out, conv_out, left_out, right_out, narrow_out, token_out,
+    tap_ref, packed_ref, in_hbm, token_ref, value_hbm,
+    low_out, gate_out, conv_out, left_out, right_out, narrow_out, token_out, value_out,
     back, out_ref, gate, mixer, conv, step, raw, padded, entry, in_ref,
     middle_low, grad_gate, grad_conv, left, right, narrow, grad_middle, mixed, low, gsel, glog, gbias, total, tail, tail_got, row_ref,
     part_ref, span_ref, wide_in, wide_out, sum_in, sum_out, states_ref, decays_ref, raw_sum, raw_rows,
-    loads, saves, passing, log_rows, relay_in, *relayed
+    loads, saves, passing, goes, comes, log_rows, relay_in, *relayed
 ):
     rows, width = step.shape
     model = up_ref.shape[1]
@@ -503,14 +540,15 @@
     scanning = [load(step_hbm, step), load(conv_hbm, conv), load(raw_hbm, raw), load(entry_hbm, entry)]
     padding = load(padded_hbm, padded)
     weights = {k: weight(k) for k in range(held, 2 * held)}
-    relay = Relay(True, log_ref, log_rows, relay_in, *relayed, chained=True)
+    relay = Relay(True, log_ref, log_rows, relay_in, *relayed, others=[{"expert": peer} for peer in expert_peers()])
 
     early[0].wait()
-    seating = seated_rows(slot_ref, rows, back.shape[0])
+    slots = slot_ref[:, 0:1]
+    seating = seated_rows(slots, rows, back.shape[0])
     chosen = chosen_ref[:, 0:1]
     along = jnp.sum(jnp.dot(seating, back[:, model:], preferred_element_type=jnp.float32), axis=1, keepdims=True)
     place = lax.broadcasted_iota(jnp.int32, (rows, LANES), 1)
-    logits = (along * chosen * (named_experts(slot_ref, rows) - probs_ref[...])).astype(jnp.bfloat16)
+    logits = (along * chosen * (named_experts(slots, rows) - probs_ref[...])).astype(jnp.bfloat16)
     grad = transposed_dot(logits, router_ref[...]) + chosen * jnp.dot(seating, back[:, :model], preferred_element_type=jnp.float32)
     narrow[...] = jnp.zeros_like(narrow)
     narrow[2 : 2 + EXPERTS, :] = column_dot(logits, normed_ref[...])
@@ -557,6 +595,7 @@
         )
 
     relay.meet()
+    trading = trade(value_hbm, value_out, goes, comes)
     staged(relay, summary, prepare, scan)
     maps = gather_maps(sum_in, rank) + gather_maps(sum_out, rank + states)
     gsel[...] = (raw_sum[...] + maps).astype(jnp.bfloat16)
@@ -637,7 +676,7 @@
     total[...] = grad_middle[...] + returned
     save(narrow, narrow_out)
     save(total, token_out)
-    for copy in saving:
+    for copy in saving + trading:
         copy.wait()
 
 
@@ -682,7 +721,7 @@
     ]
 
 
-def mixer(tokens, packed, in_weight, taps, select, step_weight, decay_log, out_weight, router, slots, seats):
+def mixer(tokens, upstream, packed, in_weight, taps, select, step_weight, decay_log, out_weight, router, routes, seats):
     rows, model = tokens.shape
     states, width = decay_log.shape
     reach = (taps.shape[0] - 1) * SEGS
@@ -705,6 +744,8 @@
         ((rows, EXPERTS), f32),
         ((rows, LANES), f32),
         ((seats, model + LANES), bf16),
+        ((rows, LANES), f32),
+        ((seats, model), bf16),
     ]
     kept = [pltpu.VMEM(dims, dtype) for dims, dtype in results]
     weights = [pltpu.VMEM((2 * width // CUT, model, CUT), bf16), pltpu.VMEM(out_weight.shape, bf16)]
@@ -712,7 +753,7 @@
     return pl.pallas_call(
         mixer_kernel,
         out_shape=tuple(shaped(*dims, dtype=dtype) for dims, dtype in results),
-        in_specs=[WHOLE] * 2 + [anywhere] + [WHOLE] * 4 + [anywhere] + [WHOLE] * 2,
+        in_specs=[WHOLE] * 3 + [anywhere] + [WHOLE] * 4 + [anywhere] + [WHOLE] * 2,
         out_specs=(anywhere,) * len(results),
         scratch_shapes=kept[:1]
         + weights
@@ -725,17 +766,19 @@
             pltpu.SemaphoreType.DMA((2 * width // CUT + 1,)),
             pltpu.SemaphoreType.DMA((len(results),)),
             pltpu.SemaphoreType.DMA((2,)),
+            pltpu.SemaphoreType.DMA((EXPERTS,)),
+            pltpu.SemaphoreType.DMA((EXPERTS,)),
         ]
         + relayed,
         compiler_params=roomy(60, collective_id=0, has_side_effects=True),
         cost_estimate=busy(rows * states * width),
         name="mixer",
-    )(tokens, packed, in_weight, taps, select, step_weight, decay_log, out_weight, router, slots)
+    )(tokens, upstream, packed, in_weight, taps, select, step_weight, decay_log, out_weight, router, routes)
 
 
 def mixer_back(
     back, slots, probs, chosen, normed, router, middle, up, out_weight, gate, mixed, conv, step, raw, selection, pre, padded, entry,
-    decay_log, step_weight, select, taps, packed, in_weight, tokens,
+    decay_log, step_weight, select, taps, packed, in_weight, tokens, value,
 ):
     rows, width = step.shape
     model = tokens.shape[1]
@@ -752,8 +795,9 @@
         ((width, LANES), f32),
         ((16, model), f32),
         ((rows, model), f32),
+        (value.shape, bf16),
     ]
-    streamed = (0, 8, 9, 10, 11, 12, 13, 15, 16, 17, 23)
+    streamed = (0, 8, 9, 10, 11, 12, 13, 15, 16, 17, 23, 25)
     kept = (
         [(back.shape, bf16), (out_weight.shape, bf16)]
         + [tall] * 5
@@ -765,7 +809,7 @@
     return pl.pallas_call(
         mixer_back_kernel,
         out_shape=tuple(shaped(*dims, dtype=dtype) for dims, dtype in results),
-        in_specs=[anywhere if k in streamed else WHOLE for k in range(25)],
+        in_specs=[anywhere if k in streamed else WHOLE for k in range(26)],
         out_specs=(anywhere,) * len(results),
         scratch_shapes=[pltpu.VMEM(dims, dtype) for dims, dtype in kept]
         + chain_scratch(states, width)
@@ -773,13 +817,14 @@
         + [wide_scratch(rows, states, 1), wide_scratch(rows, states)]
         + [pltpu.VMEM((rows, LANES), f32)] * 2
         + [pltpu.SemaphoreType.DMA((10 + 2 * held,)), pltpu.SemaphoreType.DMA((len(results),)), pltpu.SemaphoreType.DMA((2,))]
+        + [pltpu.SemaphoreType.DMA((EXPERTS,))] * 2
         + relay_scratch(),
         compiler_params=roomy(62, collective_id=1, has_side_effects=True),
         cost_estimate=busy(rows * states * width),
         name="mixer_back",
     )(
         back, slots, probs, chosen, normed, router, middle, up, out_weight, gate, mixed, conv, step, raw, selection, pre, padded, entry,
-        decay_log, step_weight, select, taps, packed, in_weight, tokens,
+        decay_log, step_weight, select, taps, packed, in_weight, tokens, value,
     )
 
 
@@ -820,7 +865,7 @@
     return jnp.einsum("tk,td->kd", left, right, preferred_element_type=jnp.float32)
 
 
-CHUNK = 1024
+CHUNK = 512
 GELU_OUT = math.sqrt(2.0 / math.pi)
 GELU_IN = 0.044715
 
@@ -842,135 +887,137 @@
     return parts
 
 
-def expert_pull_kernel(up_ref, second_ref, pull_ref):
-    pull_ref[...] = transposed_dot(up_ref[...], second_ref[...]).astype(jnp.bfloat16)
-
-
-def expert_pull(upstream, second):
+def experts_kernel(
+    leaving_hbm, up_ref, first_hbm, second_hbm, back_out, value_out, sums_out,
+    received, first, second, pull, active, grad, value, sent, back, scaled_received, scaled_up, staged_sums,
+    loads, saves, goes, comes, returns, arrives,
+):
+    rows, width = up_ref.shape
+    hidden = second.shape[0]
+    barrier = pltpu.get_barrier_semaphore()
+    for peer in expert_peers():
+        pl.semaphore_signal(barrier, inc=1, device_id={"expert": peer}, device_id_type=pl.DeviceIdType.MESH)
+    loading = [
+        pltpu.make_async_copy(second_hbm, second, loads.at[0]),
+        pltpu.make_async_copy(first_hbm, first, loads.at[1]),
+    ]
+    for copy in loading:
+        copy.start()
+    pl.semaphore_wait(barrier, EXPERTS - 1)
+    arriving = trade(leaving_hbm, received, goes, comes)
+    loading[0].wait()
+
+    def pulled(i, unused):
+        cols = pl.ds(pl.multiple_of(i * CHUNK, CHUNK), CHUNK)
+        pull[:, cols] = transposed_dot(up_ref[...], second[cols, :]).astype(jnp.bfloat16)
+        return unused
+
+    lax.fori_loop(0, hidden // CHUNK, pulled, 0)
+    loading[1].wait()
+    for copy in arriving:
+        copy.wait()
+
+    def layer(i, unused):
+        cols = pl.ds(pl.multiple_of(i * CHUNK, CHUNK), CHUNK)
+        pre = jnp.dot(received[:, :width], first[:, cols], preferred_element_type=jnp.float32)
+        square = pre * pre
+        bent = jnp.tanh(pre * (GELU_OUT + GELU_OUT * GELU_IN * square))
+        share = 0.5 + 0.5 * bent
+        slope = share + pre * (0.5 - 0.5 * bent * bent) * (GELU_OUT + 3.0 * GELU_OUT * GELU_IN * square)
+        active[:, cols] = (pre * share).astype(jnp.bfloat16)
+        grad[:, cols] = (slope * pull[:, cols].astype(jnp.float32)).astype(jnp.bfloat16)
+        return unused
+
+    lax.fori_loop(0, hidden // CHUNK, layer, 0)
+    value[...] = jnp.dot(active[...], second[...], preferred_element_type=jnp.float32).astype(jnp.bfloat16)
+    saving = [pltpu.make_async_copy(value, value_out, saves.at[0])]
+    saving[0].start()
+    sent[:, :width] = transposed_dot(grad[...], first[...]).astype(jnp.bfloat16)
+    along = jnp.sum(value[...].astype(jnp.float32) * up_ref[...].astype(jnp.float32), axis=1, keepdims=True)
+    place = lax.broadcasted_iota(jnp.int32, (rows, LANES), 1)
+    tail = jnp.zeros(place.shape, jnp.float32)
+    for k, part in enumerate(three_parts(along)):
+        tail = jnp.where(place == k, part.astype(jnp.float32), tail)
+    sent[:, width:] = tail.astype(jnp.bfloat16)
+    returning = trade(sent, back, returns, arrives)
+
+    parts = received[:, width:].astype(jnp.float32)
+    gate = parts[:, 0:1] + parts[:, 1:2] + parts[:, 2:3]
+    scaled_received[...] = (received[:, :width].astype(jnp.float32) * gate).astype(jnp.bfloat16)
+    scaled_up[...] = (up_ref[...].astype(jnp.float32) * gate).astype(jnp.bfloat16)
+    half = sums_out.shape[2]
+    pairs = hidden // half // 2
+
+    def stored(i, slot):
+        return pltpu.make_async_copy(staged_sums.at[slot], sums_out.at[pl.ds(2 * i, 2)], saves.at[1 + slot])
+
+    def sums(i, unused):
+        slot = lax.rem(i, 2)
+        cols = pl.ds(pl.multiple_of(i * 2 * half, 2 * half), 2 * half)
+
+        @pl.when(i >= 2)
+        def free():
+            stored(i - 2, slot).wait()
+
+        for which, (left, right) in enumerate(((grad, scaled_received), (active, scaled_up))):
+            total = column_dot(left[:, cols], right[...]).astype(jnp.bfloat16)
+            for k in range(2):
+                staged_sums[slot, k, which] = total[k * half : (k + 1) * half]
+        stored(i, slot).start()
+        return unused
+
+    lax.fori_loop(0, pairs, sums, 0)
+    for i in (pairs - 2, pairs - 1):
+        stored(i, i % 2).wait()
+    for copy in returning:
+        copy.wait()
+    last = pltpu.make_async_copy(back, back_out, saves.at[3])
+    last.start()
+    last.wait()
+    saving[0].wait()
+
+
+def expert_pass(leaving, upstream, first, second, owners):
     rows, width = upstream.shape
     hidden = second.shape[0]
+    wide = leaving.shape[1]
+    bf16 = jnp.bfloat16
+    half = hidden // owners
+    anywhere = pl.BlockSpec(memory_space=pl.ANY)
+
+    def kept(*dims):
+        return pltpu.VMEM(dims, bf16)
+
     return pl.pallas_call(
-        expert_pull_kernel,
-        grid=(hidden // CHUNK,),
-        out_shape=shaped(rows, hidden, dtype=jnp.bfloat16),
-        in_specs=[pl.BlockSpec((rows, width), lambda i: (0, 0)), pl.BlockSpec((CHUNK, width), lambda i: (i, 0))],
-        out_specs=pl.BlockSpec((rows, CHUNK), lambda i: (0, i)),
-        compiler_params=roomy(60),
-        cost_estimate=pl.CostEstimate(flops=2 * rows * hidden * width, bytes_accessed=2 * (width + rows) * hidden, transcendentals=0),
-        name="expert_pull",
-    )(upstream, second)
-
-
-def expert_kernel(got_ref, up_ref, pull_ref, first_ref, second_ref, active_ref, grad_ref, value_ref, sent_ref, value, sent):
-    step, last = pl.program_id(0), pl.num_programs(0) - 1
-    width = up_ref.shape[1]
-    first = first_ref[...]
-    pre = jnp.dot(got_ref[:, :width], first, preferred_element_type=jnp.float32)
-    square = pre * pre
-    bent = jnp.tanh(pre * (GELU_OUT + GELU_OUT * GELU_IN * square))
-    share = 0.5 + 0.5 * bent
-    active = (pre * share).astype(jnp.bfloat16)
-    slope = share + pre * (0.5 - 0.5 * bent * bent) * (GELU_OUT + 3.0 * GELU_OUT * GELU_IN * square)
-    grad = (slope * pull_ref[...].astype(jnp.float32)).astype(jnp.bfloat16)
-    active_ref[...] = active
-    grad_ref[...] = grad
-    more_value = jnp.dot(active, second_ref[...], preferred_element_type=jnp.float32)
-    more_sent = transposed_dot(grad, first)
-
-    @pl.when(step == 0)
-    def begin():
-        value[...] = more_value
-        sent[...] = more_sent
-
-    @pl.when(step > 0)
-    def go_on():
-        value[...] += more_value
-        sent[...] += more_sent
-
-    @pl.when(step == last)
-    def finish():
-        low = value[...].astype(jnp.bfloat16)
-        value_ref[...] = low
-        sent_ref[:, :width] = sent[...].astype(jnp.bfloat16)
-        along = jnp.sum(low.astype(jnp.float32) * up_ref[...].astype(jnp.float32), axis=1, keepdims=True)
-        place = lax.broadcasted_iota(jnp.int32, (sent_ref.shape[0], LANES), 1)
-        tail = jnp.zeros(place.shape, jnp.float32)
-        for k, part in enumerate(three_parts(along)):
-            tail = jnp.where(place == k, part.astype(jnp.float32), tail)
-        sent_ref[:, width:] = tail.astype(jnp.bfloat16)
-
-
-def expert_layer(received, upstream, pull, first, second):
-    rows, width = upstream.shape
-    hidden = second.shape[0]
-    wide = received.shape[1]
-
-    def fixed(cols):
-        return pl.BlockSpec((rows, cols), lambda i: (0, 0))
-
-    chunk = pl.BlockSpec((rows, CHUNK), lambda i: (0, i))
-    return pl.pallas_call(
-        expert_kernel,
-        grid=(hidden // CHUNK,),
+        experts_kernel,
         out_shape=(
-            shaped(rows, hidden, dtype=jnp.bfloat16),
-            shaped(rows, hidden, dtype=jnp.bfloat16),
-            shaped(rows, width, dtype=jnp.bfloat16),
-            shaped(rows, wide, dtype=jnp.bfloat16),
+            shaped(rows, wide, dtype=bf16),
+            shaped(rows, width, dtype=bf16),
+            shaped(owners, 2, half, width, dtype=bf16),
         ),
-        in_specs=[
-            fixed(wide),
-            fixed(width),
-            chunk,
-            pl.BlockSpec((width, CHUNK), lambda i: (0, i)),
-            pl.BlockSpec((CHUNK, width), lambda i: (i, 0)),
-        ],
-        out_specs=(chunk, chunk, fixed(width), fixed(wide)),
-        scratch_shapes=[pltpu.VMEM((rows, width), jnp.float32)] * 2,
-        compiler_params=roomy(60),
-        cost_estimate=pl.CostEstimate(flops=6 * rows * hidden * width, bytes_accessed=4 * hidden * (width + rows), transcendentals=rows * hidden),
-        name="expert_layer",
-    )(received, upstream, pull, first, second)
-
-
-def expert_sums_kernel(hidden_ref, received_ref, active_ref, up_ref, out_ref, scaled_received, scaled_up):
-    pair = out_ref.shape[0]
-    half = out_ref.shape[2]
-    width = up_ref.shape[1]
-
-    @pl.when(pl.program_id(0) == 0)
-    def scale():
-        parts = received_ref[:, width:].astype(jnp.float32)
-        gate = parts[:, 0:1] + parts[:, 1:2] + parts[:, 2:3]
-        scaled_received[...] = (received_ref[:, :width].astype(jnp.float32) * gate).astype(jnp.bfloat16)
-        scaled_up[...] = (up_ref[...].astype(jnp.float32) * gate).astype(jnp.bfloat16)
-
-    for which, (left_ref, right_ref) in enumerate(((hidden_ref, scaled_received), (active_ref, scaled_up))):
-        total = column_dot(left_ref[...], right_ref[...]).astype(jnp.bfloat16)
-        for i in range(pair):
-            out_ref[i, which] = total[i * half : (i + 1) * half]
-
-
-def expert_sums(grad_hidden, received, activated, upstream, owners):
-    rows, hidden = grad_hidden.shape
-    width = upstream.shape[1]
-    pair = 2
-    chunk = pl.BlockSpec((rows, pair * hidden // owners), lambda i: (0, i))
-
-    def fixed(cols):
-        return pl.BlockSpec((rows, cols), lambda i: (0, 0))
-
-    return pl.pallas_call(
-        expert_sums_kernel,
-        grid=(owners // pair,),
-        out_shape=shaped(owners, 2, hidden // owners, width, dtype=jnp.bfloat16),
-        in_specs=[chunk, fixed(received.shape[1]), chunk, fixed(width)],
-        out_specs=pl.BlockSpec((pair, 2, hidden // owners, width), lambda i: (i, 0, 0, 0)),
-        scratch_shapes=[pltpu.VMEM((rows, width), jnp.bfloat16)] * 2,
-        compiler_params=roomy(60),
-        cost_estimate=pl.CostEstimate(flops=4 * rows * hidden * width, bytes_accessed=4 * hidden * (width + rows), transcendentals=0),
-        name="expert_sums",
-    )(grad_hidden, received, activated, upstream)
+        in_specs=[anywhere, WHOLE, anywhere, anywhere],
+        out_specs=(anywhere,) * 3,
+        scratch_shapes=[
+            kept(rows, wide),
+            kept(width, hidden),
+            kept(hidden, width),
+            kept(rows, hidden),
+            kept(rows, hidden),
+            kept(rows, hidden),
+            kept(rows, width),
+            kept(rows, wide),
+            kept(rows, wide),
+            kept(rows, width),
+            kept(rows, width),
+            kept(2, 2, 2, half, width),
+            pltpu.SemaphoreType.DMA((2,)),
+            pltpu.SemaphoreType.DMA((4,)),
+        ]
+        + [pltpu.SemaphoreType.DMA((EXPERTS,))] * 4,
+        compiler_params=roomy(60, collective_id=3, has_side_effects=True),
+        cost_estimate=pl.CostEstimate(flops=12 * rows * hidden * width, bytes_accessed=8 * hidden * width, transcendentals=rows * hidden),
+        name="experts",
+    )(leaving, upstream, first, second)
 
 
 ORDERS = ("xyz", "yzx", "zxy")
@@ -978,7 +1025,8 @@
 
 
 def shares_kernel(
-    conv_cols, gate_cols, token_ref, out_cols, middle_ref, left_ref, right_ref, narrow_ref, sum_ref, in_ref, out_ref, made, taken,
+    conv_cols, gate_cols, token_ref, out_cols, middle_ref, left_ref, right_ref, narrow_ref,
+    in_out, out_out, left_out, right_out, narrow_out, sum_ref, in_ref, out_ref, made, taken,
     half_a, half_b, half_c, one_a, one_b, one_c, sends, arrivals):
     seq, expert = lax.axis_index("seq"), lax.axis_index("expert")
     core = lax.rem(expert, 2)
@@ -1027,7 +1075,17 @@
 
         lax.fori_loop(0, source.shape[1] // LANES, turn_over, 0)
 
-    pending = {}
+    halves, ones = (half_a, half_b, half_c), (one_a, one_b, one_c)
+    pending, holding = {}, {}
+
+    def set_out(L):
+        for q in range(4):
+            for copy in pending[L, q]:
+                copy.wait()
+            add(taken.at[L, q], made.at[L, 4 * core + q], 64)
+            holding[L, q] = taken.at[L, q]
+            pending[L, q] = start_halves(L, q, 0, holding[L, q], halves, place, flip, device, send)
+
     for L, order in enumerate(ORDERS):
         lanes = pl.ds(L * third, third)
         narrow = narrow_ref[:, lanes].astype(jnp.bfloat16)
@@ -1065,14 +1123,9 @@
                 send(made.at[L, 4 * (1 - core) + q], taken.at[L, q], device(core=1 - core), (L, q), 0)
             ]
 
-    halves, ones = (half_a, half_b, half_c), (one_a, one_b, one_c)
-    holding = {}
-    for L, q in streams:
-        for copy in pending[L, q]:
-            copy.wait()
-        add(taken.at[L, q], made.at[L, 4 * core + q], 64)
-        holding[L, q] = taken.at[L, q]
-        pending[L, q] = start_halves(L, q, 0, holding[L, q], halves, place, flip, device, send)
+        if L:
+            set_out(L - 1)
+    set_out(len(ORDERS) - 1)
     for turn in range(3):
         unit = 16 >> (2 * turn)
         for L, q in streams:
@@ -1099,6 +1152,17 @@
                 sum_ref[4 * core + q, :, L * third : (L + 1) * third] = whole
     here = sum_ref.at[pl.ds(4 * core, 4)]
     send(here, here, device(core=1 - core), (0, 0), 10).wait()
+    whole = jnp.concatenate([sum_ref[q] for q in range(8)], axis=0)
+    last = jnp.concatenate([whole[112:120, k * LANES : (k + 1) * LANES] for k in range(whole.shape[1] // LANES)], axis=0)
+    narrow_out[...] = jnp.concatenate([whole[120:128], whole[108:112], whole[108:112]], axis=0)
+    for c in range(2):
+
+        @pl.when(core == c)
+        def pick(c=c):
+            in_out[...] = whole[36 * c : 36 * c + 36]
+            out_out[...] = whole[72 + 18 * c : 90 + 18 * c]
+            left_out[...] = last[18 * c : 18 * c + 18]
+            right_out[...] = last[36 + 18 * c : 54 + 18 * c]
 
 
 def start_halves(L, q, turn, source, halves, place, flip, device, send):
@@ -1124,10 +1188,11 @@
 
     return pl.pallas_call(
         shares_kernel,
-        out_shape=shaped(8, PIECE, width),
+        out_shape=(shaped(36, width), shaped(18, width), shaped(18, LANES), shaped(18, LANES), shaped(16, width)),
         in_specs=[WHOLE] * 8,
-        out_specs=WHOLE,
-        scratch_shapes=[pltpu.VMEM((2 * inner, rows), jnp.bfloat16), pltpu.VMEM((inner, rows), jnp.bfloat16)]
+        out_specs=(WHOLE,) * 5,
+        scratch_shapes=[pltpu.VMEM((8, PIECE, width), jnp.float32)]
+        + [pltpu.VMEM((2 * inner, rows), jnp.bfloat16), pltpu.VMEM((inner, rows), jnp.bfloat16)]
         + [slots(8, 64), slots(4, 64)]
         + [slots(4, 2, 16 >> (2 * turn)) for turn in range(3)]
         + [slots(4, 16 >> (2 * turn)) for turn in range(3)]
@@ -1158,7 +1223,7 @@
 ):
     bf16, f32 = jnp.bfloat16, jnp.float32
     stream = segmented(tokens[0])
-    routes = segmented(expert_index[0])[:, 0]
+    routes = segmented(expert_index[0])
     upstream = segmented(cotangent[0])
     row_count, model_width = stream.shape
     seat_count = 2 * row_count
@@ -1166,74 +1231,33 @@
     rank = step_weight.shape[0]
     states = decay_log.shape[0]
     taps = conv_weight.shape[0]
-    expert_count = router_weight.shape[1]
-    capacity = 2 * row_count // expert_count
     seqs, experts = lax.axis_size("seq"), lax.axis_size("expert")
-    reach = (taps - 1) * SEGS
-
-    picks = (routes[:, None] == jnp.arange(expert_count, dtype=jnp.int32)[None, :]).astype(bf16)
-    earlier = jnp.arange(row_count)[:, None] > jnp.arange(row_count)[None, :]
-    ahead = product(earlier.astype(bf16), picks)
-    chosen = picks.astype(f32)
-    slot_index = routes * capacity + jnp.sum(ahead * chosen, axis=1).astype(jnp.int32)
-    seats = jnp.arange(expert_count * capacity, dtype=jnp.int32)
-    placing = (seats[:, None] == slot_index[None, :]).astype(bf16)
-
-    def seated(rows):
-        return product(placing, rows).astype(bf16)
-
-    def swapped(rows):
-        parts = rows.reshape(expert_count, capacity, -1)
-        parts = lax.all_to_all(parts, "expert", split_axis=0, concat_axis=0, tiled=True)
-        return parts.reshape(expert_count * capacity, -1)
-
-    def unseated(rows):
-        return jnp.einsum("st,sd->td", placing, rows, preferred_element_type=f32)
-
-    upstream_there = swapped(seated(upstream))
-
     packed = jnp.concatenate([conv_bias, step_bias, skip_gain, first_gain, second_gain]).reshape(4, inner)
-    slot_column = slot_index[:, None]
     (
         normed_in, gate_input, padded, preact, conv_out, step_raw, step_size, selection, first, mixer_out, gated,
-        middle, normed_mid, router_probs, gate_wide, leaving,
+        middle, normed_mid, router_probs, gate_wide, leaving, slots, upstream_there,
     ) = mixer(
-        stream, packed, in_weight, conv_weight, select_weight, step_weight, decay_log, out_weight, router_weight, slot_column, seat_count
+        stream, upstream, packed, in_weight, conv_weight, select_weight, step_weight, decay_log, out_weight, router_weight, routes, seat_count
     )
-    leaving, upstream_there = lax.optimization_barrier((leaving, upstream_there))
-    received = swapped(leaving)
-    pull = expert_pull(upstream_there, expert_second[0])
-    activated, grad_hidden, value_there, grad_there = expert_layer(
-        received, upstream_there, pull, expert_first[0], expert_second[0]
-    )
-    back = swapped(grad_there)
-    expert_grads = expert_sums(grad_hidden, received, activated, upstream_there, seqs)
-    expert_grads, value_there, back = lax.optimization_barrier((expert_grads, value_there, back))
-    value_home = swapped(value_there)
+    back, value_there, expert_grads = expert_pass(leaving, upstream_there, expert_first[0], expert_second[0], seqs)
     expert_share = lax.psum_scatter(
         expert_grads.reshape(-1, model_width), "seq", scatter_dimension=0, tiled=True
     ).reshape(2, -1, model_width)
-    middle_low, grad_gate_input, grad_conv_input, left, right, narrow, grad_tokens = mixer_back(
-        back, slot_column, router_probs, gate_wide, normed_mid, router_weight, middle, upstream, out_weight, gate_input, mixer_out, conv_out,
-        step_size, step_raw, selection, preact, padded, first, decay_log, step_weight, select_weight, conv_weight, packed, in_weight, stream,
+    middle_low, grad_gate_input, grad_conv_input, left, right, narrow, grad_tokens, value_home = mixer_back(
+        back, slots, router_probs, gate_wide, normed_mid, router_weight, middle, upstream, out_weight, gate_input, mixer_out, conv_out,
+        step_size, step_raw, selection, preact, padded, first, decay_log, step_weight, select_weight, conv_weight, packed, in_weight, stream, value_there,
     )
-    middle_low, value_home = lax.optimization_barrier((middle_low, value_home))
-    mixed = middle + gate_wide[:, 0:1] * unseated(value_home)
+    placing = (slots[:, 0:1] == jnp.arange(seat_count, dtype=f32)[None, :]).astype(bf16)
+    mixed = middle + gate_wide[:, 0:1] * product(placing, value_home)
 
     devices = seqs * experts
     each, fewer = inner // devices, model_width // devices
-    grad_conv_input, expert_share = lax.optimization_barrier((grad_conv_input, expert_share))
-    sums = shares(grad_conv_input, grad_gate_input, normed_in, gated, middle_low, left, right, narrow)
-    sums = sums.reshape(-1, model_width)
-    core = lax.axis_index("expert") % 2
-    in_share = lax.dynamic_slice_in_dim(sums, 2 * each * core, 2 * each)
-    out_share = lax.dynamic_slice_in_dim(sums, 4 * each + each * core, each)
-    small = sums[112:120].reshape(8, -1, LANES).transpose(1, 0, 2).reshape(2, 2 * each, LANES)
-    small = lax.dynamic_slice_in_dim(small, each * core, each, axis=1)
-    rows_sum = small[0, :, rank + 2 * states :]
+    in_share, out_share, left, right, narrow = shares(
+        grad_conv_input, grad_gate_input, normed_in, gated, middle_low, left, right, narrow
+    )
+    rows_sum = left[:, rank + 2 * states :]
     owner = lax.axis_index("seq") * experts + lax.axis_index("expert")
-    narrow_sum = jnp.concatenate([sums[120:128], sums[108:110]])
-    narrow_sum = lax.dynamic_slice_in_dim(narrow_sum, owner * fewer, fewer, axis=1)
+    narrow_sum = lax.dynamic_slice_in_dim(narrow, owner * fewer, fewer, axis=1)
     return (
         in_order(mixed.astype(bf16))[None],
         in_order(grad_tokens)[None],
@@ -1241,14 +1265,14 @@
         in_share.T,
         rows_sum[:, states : states + taps].T,
         rows_sum[:, states + taps],
-        small[0, :, : rank + 2 * states],
-        small[1, :, :rank].T,
+        left[:, : rank + 2 * states],
+        right[:, :rank].T,
         rows_sum[:, states + taps + 1],
         rows_sum[:, :states].T,
         rows_sum[:, states + taps + 2],
         out_share,
         narrow_sum[1],
-        narrow_sum[2:].T,
+        narrow_sum[2:10].T,
         expert_share[0].T.astype(f32)[None],
         expert_share[1].astype(f32)[None],
     )

time: 338 us -> 317 us (0.938)
  Pallas kernels: 252 us -> 276 us
  starting transfers between devices: 22.6 us -> 0.04 us
  waiting for transfers between devices: 21.2 us -> 0.02 us
    all_to_all x4 -> x0, starting transfers between devices: 22.6 us -> none  [swapped(): lax.all_to_all(parts, 'expert', split_axis=0, concat_axis=0, tiled=True)]
    pallas_call x4 -> x2, Pallas kernels: 120 us -> 134 us  [the longest x1 76.5 us: shares(): pl.pallas_call(shares_kernel, out_shape=(shaped(36, width), shaped(18, wi...]
    all_to_all x4 -> x0, waiting for transfers between devices: 12.5 us -> none  [swapped(): lax.all_to_all(parts, 'expert', split_axis=0, concat_axis=0, tiled=True)]
    pallas_call x1, Pallas kernels: 81.2 us -> 91 us  [mixer_back(): pl.pallas_call(mixer_back_kernel, out_shape=tuple((shaped(*dims, dtype=dt...]
    reduce_scatter x1, waiting for transfers between devices: 8.65 us -> 0.01 us  [local(): lax.psum_scatter(expert_grads.reshape(-1, model_width), 'seq', scatter_di...]
    unnamed x41 -> x48, local copies, waits for them, and re-layouts: 8.01 us -> 6.42 us
  transfers between devices with their start and end apart: 5 -> 1, of which waited for: 3 -> 0; matrix products, arithmetic and copies ran while one was open for 3% -> 3% of each run, Pallas kernels for 46% -> 53%
where the time goes in v1:
time: 317 us; the launch traced here: 313 us
  Pallas kernels  276 us (87%)
  local copies, waits for them, and re-layouts  19 us (6%)
  between operations  14.5 us (5%)
  other arithmetic  3.17 us (1%)
    pallas_call x1, Pallas kernels, mixer_back(): pl.pallas_call(mixer_back_kernel, out_shape=tuple((shaped(*dims, dtype=dt...  91 us
    pallas_call x1, Pallas kernels, shares(): pl.pallas_call(shares_kernel, out_shape=(shaped(36, width), shaped(18, wi...  76.5 us
    pallas_call x1, Pallas kernels, expert_pass(): pl.pallas_call(experts_kernel, out_shape=(shaped(rows, wide, dtype=bf16),...  57.9 us
    pallas_call x1, Pallas kernels, mixer(): pl.pallas_call(mixer_kernel, out_shape=tuple((shaped(*dims, dtype=dtype)...  50.6 us
    unnamed x48, local copies, waits for them, and re-layouts  6.42 us
  transfers between devices with their start and end apart: 1, of which 0 were waited for; matrix products, arithmetic and copies ran while one was open for 3% of the time, Pallas kernels for 53%

profile of v1, /device:TPU:1, one launch (start us, length us, event | category | flops | bytes accessed | tf_op | source)
XLA Modules:
  0.0 313.3 jit_solution(5661980978592259929)
XLA Ops:
  7.3 2.1 copy.58
  9.5 1.0 copy.59
  10.5 1.1 copy.47.select_ref
  11.5 0.9 copy.48.router_ref
  12.5 0.6 reshape.63.row_ref.packed_ref
  13.6 0.7 reduce.13
  14.5 0.8 reshape.70.route_ref
  15.2 50.6 %mixer.1 = (bf16[256,1152]{1,0:T(8,128)(2,1)}, f32[256,2304]{1,0:T(8,128)}, f32[280,2304]{1,0:T(8,128)}, f32[256,2304]{1,0:T(8,128)}, f32[256,2304]{1,0:T(8,128)...) custom-call(bf16[256,1152]{1,0:T(8,128)(2,1)} %bitcast.59, ...), custom_call_target="tpu_custom_call" | custom-call | flops 38654705664 | bytes 150994944 | tf_op jit(solution)/shard_map/mixer/pallas_call | solution.py:753
  65.9 57.9 %experts.1 = (bf16[512,1280]{1,0:T(8,128)(2,1)}, bf16[512,1152]{1,0:T(8,128)(2,1)}, bf16[16,2,192,1152]{3,2,1,0:T(8,128)(2,1)}) custom-call(bf16[512,1280]{1,0:T(8,128)(2,1)} %get-tuple-element.53.leaving_hbm, bf16[512,1152]{1,0:T(8,128)(2,1)} %get-tuple-element.54.up_ref, bf16[1152,3072]{1,0:T(8,128)(2,1)} %bitcast.65, bf16[3072,1152]{1,0:T(8,128)(2,1)} %bitcast.66), custom_call_target="tpu_custom_call" | custom-call | flops 21743271936 | bytes 28311552 | tf_op jit(solution)/shard_map/experts/pallas_call | solution.py:991
  123.8 91.0 %mixer_back.1 = (bf16[256,1152]{1,0:T(8,128)(2,1)}, bf16[256,2304]{1,0:T(8,128)(2,1)}, bf16[256,2304]{1,0:T(8,128)(2,1)}, f32[2304,128]{1,0:T(8,128)}, f32[2304,...) custom-call(bf16[512,1280]{1,0:T(8,128)(2,1)} %get-tuple-element.55.back_hbm, ...), custom_call_target="tpu_custom_call" | custom-call | flops 38654705664 | bytes 150994944 | tf_op jit(solution)/shard_map/mixer_back/pallas_call | solution.py:809
  214.9 76.5 %shares.1 = (f32[36,1152]{1,0:T(8,128)}, f32[18,1152]{1,0:T(8,128)}, f32[18,128]{1,0:T(8,128)}, f32[18,128]{1,0:T(8,128)}, f32[16,1152]{1,0:T(8,128)}) custom-call(bf16[256,2304]{1,0:T(8,128)(2,1)} %get-tuple-element.70.conv_cols, bf16[256,2304]{1,0:T(8,128)(2,1)} %get-tuple-element.71.gate_cols, bf16[256,1152]{1,0:T(8,128)(2,1)} %get-tuple-element.72.token_ref, ...), custom_call_target="tpu_custom_call" | custom-call | tf_op jit(solution)/shard_map/shares/pallas_call | solution.py:1189
  291.4 0.8 slice_bitcast_fusion.1
  292.2 0.7 copy.55
  292.8 0.8 slice_bitcast_fusion.3
  293.6 0.7 copy.54
  295.0 0.9 copy.52
  296.5 1.2 copy.53
  297.7 1.4 dynamic-slice_bitcast_fusion.1
  299.1 1.4 dynamic-slice_bitcast_fusion
  300.5 0.7 slice_reduce_fusion.2
  301.2 0.6 slice_bitcast_fusion.2
  301.8 2.5 fusion.3
  304.3 0.7 copy.68
  305.6 0.6 copy.70
  (51 shorter events, 2.7 us)
Async XLA Ops:
  7.2 2.2 copy-start.3
  7.2 294.6 %reduce-scatter.2.cloned.1.call-start = ((), (), s32[]{:S(2)}) async-start(), calls=%async_computation.1 | async-start | bytes 15040512 | tf_op jit(solution)/shard_map/reduce_scatter | solution.py:1243
  7.2 3.2 %copy-start.4 = (bf16[2304,104]{0,1:T(8,128)(2,1)S(1)}, bf16[2304,104]{0,1:T(8,128)(2,1)}, u32[]{:S(2)}) copy-start(bf16[2304,104]{0,1:T(8,128)(2,1)} %param.24) | copy-start | bytes 1437700
  9.4 2.1 copy-start.10
  9.4 3.0 copy-start.11
  9.4 3.0 copy-start.12
  9.4 3.0 copy-start.13
  9.4 3.0 copy-start.15
  9.4 3.0 copy-start.16
  9.4 4.2 %copy-start.17 = (s32[1,256,1]{1,2,0:T(1,128)S(1)}, s32[1,256,1]{1,2,0:T(1,128)}, u32[]{:S(2)}) copy-start(s32[1,256,1]{1,2,0:T(1,128)} %param.18) | copy-start | bytes 3076
  214.8 79.5 %copy-start.7 = (f32[256,128]{1,0:T(8,128)S(1)}, f32[256,128]{1,0:T(8,128)}, u32[]{:S(2)}) copy-start(f32[256,128]{1,0:T(8,128)} %get-tuple-element.51.chosen_ref) | copy-start | bytes 393220
  214.8 79.5 %copy-start.8 = (f32[256,128]{1,0:T(8,128)S(1)}, f32[256,128]{1,0:T(8,128)}, u32[]{:S(2)}) copy-start(f32[256,128]{1,0:T(8,128)} %get-tuple-element.52.slot_ref) | copy-start | bytes 393220
  214.8 79.6 %copy-start = (f32[256,1152]{1,0:T(8,128)S(1)}, f32[256,1152]{1,0:T(8,128)}, u32[]{:S(2)}) copy-start(f32[256,1152]{1,0:T(8,128)} %get-tuple-element.50.middle_ref) | copy-start | bytes 3538948
  214.8 79.6 %copy-start.2 = (bf16[512,1152]{1,0:T(8,128)(2,1)S(1)}, bf16[512,1152]{1,0:T(8,128)(2,1)}, u32[]{:S(2)}) copy-start(bf16[512,1152]{1,0:T(8,128)(2,1)} %get-tuple-element.68) | copy-start | bytes 3538948
  295.0 1.5 copy-start.1
  296.5 4.0 %copy-start.5 = (f32[18,128]{1,0:T(8,128)S(1)}, f32[18,128]{1,0:T(8,128)}, u32[]{:S(2)}) copy-start(f32[18,128]{1,0:T(8,128)} %get-tuple-element.80) | copy-start | bytes 27652
  296.5 4.7 %copy-start.14 = (f32[18,128]{1,0:T(8,128)S(1)}, f32[18,128]{1,0:T(8,128)}, u32[]{:S(2)}) copy-start(f32[18,128]{1,0:T(8,128)} %get-tuple-element.81) | copy-start | bytes 27652
  301.8 2.5 copy-start.6
  301.8 3.8 %copy-start.9 = (f32[18,1152]{1,0:T(8,128)S(1)}, f32[18,1152]{1,0:T(8,128)}, u32[]{:S(2)}) copy-start(f32[18,1152]{1,0:T(8,128)} %get-tuple-element.152) | copy-start | bytes 248836
Sparse Core Ops, SparseCore 0:
  124.0 100.7 reduce-scatter.1

commit v2 on v1

--- a/solution.py
+++ b/solution.py
@@ -353,19 +353,28 @@
     return jnp.where(seat == slots, 1.0, 0.0).astype(jnp.bfloat16)
 
 
+def order_ones(rows, back):
+    row, token = lax.broadcasted_iota(jnp.int32, (rows, rows), 0), lax.broadcasted_iota(jnp.int32, (rows, rows), 1)
+    if back:
+        row, token = token, row
+    same = token == lax.rem(row, SEGS) * (rows // SEGS) + lax.div(row, SEGS)
+    return jnp.where(same, 1.0, 0.0).astype(jnp.bfloat16)
+
+
 def slots_of(routes, rows):
     expert = lax.broadcasted_iota(jnp.int32, (rows, EXPERTS), 1)
-    named = jnp.where(expert == routes, 1.0, 0.0)
+    named = jnp.where(lax.broadcasted_iota(jnp.int32, (EXPERTS, rows), 0) == routes, 1.0, 0.0).astype(jnp.bfloat16)
+    named = transposed_dot(order_ones(rows, False), named)
     later = lax.broadcasted_iota(jnp.int32, (rows, rows), 0) > lax.broadcasted_iota(jnp.int32, (rows, rows), 1)
     ahead = jnp.dot(jnp.where(later, 1.0, 0.0).astype(jnp.bfloat16), named.astype(jnp.bfloat16), preferred_element_type=jnp.float32)
     return jnp.sum(named * (ahead + (expert * CAPACITY).astype(jnp.float32)), axis=1, keepdims=True)
 
 
 def mixer_kernel(
-    token_ref, up_ref, row_ref, in_hbm, tap_ref, select_ref, step_weight_ref, log_ref, out_hbm, router_ref, route_ref,
+    token_in, up_in, tap_bias_in, step_bias_in, skip_in, gain_in, second_gain_in, in_hbm, tap_ref, select_ref, step_weight_ref, log_ref, out_hbm, router_ref, route_ref,
     normed_out, gate_out, padded_out, pre_out, conv_out, raw_out, step_out, sel_out, entry_out, mixer_out, gated_out,
-    middle_out, normed_mid_out, probs_out, chosen_out, leaving_out, slot_out, up_out,
-    normed, in_ref, out_ref, padded, gate, pre, conv, raw, step, sel, entry, mixer, gated, middle, normed_mid, probs, chosen, leaving, slots, up_seated,
+    middle_out, normed_mid_out, probs_out, chosen_out, leaving_out, slot_out, up_out, token_out, up_order_out, row_out,
+    normed, in_ref, out_ref, padded, gate, pre, conv, raw, step, sel, entry, mixer, gated, middle, normed_mid, probs, chosen, leaving, slots, up_seated, token_ref, up_ref, row_ref,
     tail, tail_got, part_ref, span_ref, wide_in, wide_out, loads, saves, passing, goes, comes, log_rows, relay_in, *relayed
 ):
     rows, width = step.shape
@@ -392,7 +401,16 @@
 
     relay = Relay(False, log_ref, log_rows, relay_in, *relayed, others=[{"expert": peer} for peer in expert_peers()])
 
-    stream = token_ref[...].astype(jnp.float32)
+    for k, vector in enumerate((tap_bias_in, step_bias_in, skip_in)):
+        row_ref[k : k + 1, :] = vector[...][None, :]
+    row_ref[3:4, :model] = gain_in[...][None, :]
+    row_ref[3:4, model:] = second_gain_in[...][None, :]
+    row_ref[4:, :] = jnp.zeros_like(row_ref[4:, :])
+    save(row_ref, row_out)
+    ordering = order_ones(rows, False)
+    stream = jnp.dot(ordering, token_in[...], preferred_element_type=jnp.float32)
+    token_ref[...] = stream.astype(jnp.bfloat16)
+    save(token_ref, token_out)
     normed[...] = (stream * rms_scale(stream) * gain_ref[...]).astype(jnp.bfloat16)
     save(normed, normed_out)
     for k in range(pieces // 2):
@@ -406,6 +424,8 @@
     slots[...] = jnp.broadcast_to(slot, slots.shape)
     save(slots, slot_out)
     seating = seated_rows(slot, rows, leaving.shape[0])
+    up_ref[...] = jnp.dot(ordering, up_in[...], preferred_element_type=jnp.float32).astype(jnp.bfloat16)
+    save(up_ref, up_order_out)
     up_seated[...] = column_dot(seating, up_ref[...]).astype(jnp.bfloat16)
     relay.meet()
     handing = pltpu.make_async_remote_copy(
@@ -438,7 +458,7 @@
         pre[:, lanes] = value
         value = value * jax.nn.sigmoid(value)
         conv[:, lanes] = value
-        sel[:, :SELECTED] += jnp.dot(value.astype(jnp.bfloat16), select_ref[lanes, :], preferred_element_type=jnp.float32)
+        sel[:, :SELECTED] += transposed_dot(value.astype(jnp.bfloat16), select_ref[:, lanes])
         return unused
 
     lax.fori_loop(0, blocks, convolve, 0)
@@ -485,7 +505,7 @@
     save(middle, middle_out)
     normed_mid[...] = (value * rms_scale(value) * second_gain_ref[...]).astype(jnp.bfloat16)
     save(normed_mid, normed_mid_out)
-    logits = jnp.dot(normed_mid[...], router_ref[...], preferred_element_type=jnp.float32)
+    logits = transposed_dot(normed_mid[...], router_ref[...])
     grown = jnp.exp(logits - jnp.max(logits, axis=1, keepdims=True))
     probs[...] = grown / jnp.sum(grown, axis=1, keepdims=True)
     save(probs, probs_out)
@@ -549,12 +569,12 @@
     along = jnp.sum(jnp.dot(seating, back[:, model:], preferred_element_type=jnp.float32), axis=1, keepdims=True)
     place = lax.broadcasted_iota(jnp.int32, (rows, LANES), 1)
     logits = (along * chosen * (named_experts(slots, rows) - probs_ref[...])).astype(jnp.bfloat16)
-    grad = transposed_dot(logits, router_ref[...]) + chosen * jnp.dot(seating, back[:, :model], preferred_element_type=jnp.float32)
+    grad = jnp.dot(logits, router_ref[...], preferred_element_type=jnp.float32) + chosen * jnp.dot(seating, back[:, :model], preferred_element_type=jnp.float32)
     narrow[...] = jnp.zeros_like(narrow)
-    narrow[2 : 2 + EXPERTS, :] = column_dot(logits, normed_ref[...])
+    narrow[:EXPERTS, :] = column_dot(logits, normed_ref[...])
     value = middle_ref[...]
     returned, gained = rms_back(value, rms_scale(value), second_gain_ref[...], grad)
-    narrow[1:2, :] = gained[None, :]
+    narrow[EXPERTS + 1 : EXPERTS + 2, :] = gained[None, :]
     value = up_ref[...].astype(jnp.float32) + returned
     grad_middle[...] = value
     middle_low[...] = value.astype(jnp.bfloat16)
@@ -610,7 +630,7 @@
     def convolve_back(b, unused):
         lanes = lanes_of(b)
         around, kept = mixed[:, lanes], conv[:, lanes]
-        grown = transposed_dot(gsel[:, :SELECTED], select_ref[lanes, :]) + gconv[:, lanes] + skip_ref[:, lanes] * around
+        grown = jnp.dot(gsel[:, :SELECTED], select_ref[:, lanes], preferred_element_type=jnp.float32) + gconv[:, lanes] + skip_ref[:, lanes] * around
         grown = grown * silu_slope(pre[:, lanes])
         gconv[:, lanes] = grown
         row_ref[:states, :] = glog[:, lanes]
@@ -672,9 +692,11 @@
     save(grad_conv, conv_out)
     stream = token_ref[...].astype(jnp.float32)
     returned, gained = rms_back(stream, rms_scale(stream), gain_ref[...], total[...])
-    narrow[0:1, :] = gained[None, :]
-    total[...] = grad_middle[...] + returned
+    narrow[EXPERTS : EXPERTS + 1, :] = gained[None, :]
     save(narrow, narrow_out)
+    value = grad_middle[...] + returned
+    ordering = order_ones(rows, True)
+    total[...] = sum(jnp.dot(ordering, part, preferred_element_type=jnp.float32) for part in three_parts(value))
     save(total, token_out)
     for copy in saving + trading:
         copy.wait()
@@ -721,7 +743,7 @@
     ]
 
 
-def mixer(tokens, upstream, packed, in_weight, taps, select, step_weight, decay_log, out_weight, router, routes, seats):
+def mixer(tokens, upstream, tap_bias, step_bias, skip, gain, second_gain, in_weight, taps, select, step_weight, decay_log, out_weight, router, routes, seats):
     rows, model = tokens.shape
     states, width = decay_log.shape
     reach = (taps.shape[0] - 1) * SEGS
@@ -746,6 +768,9 @@
         ((seats, model + LANES), bf16),
         ((rows, LANES), f32),
         ((seats, model), bf16),
+        ((rows, model), bf16),
+        ((rows, model), bf16),
+        ((SEGS, width), f32),
     ]
     kept = [pltpu.VMEM(dims, dtype) for dims, dtype in results]
     weights = [pltpu.VMEM((2 * width // CUT, model, CUT), bf16), pltpu.VMEM(out_weight.shape, bf16)]
@@ -753,7 +778,7 @@
     return pl.pallas_call(
         mixer_kernel,
         out_shape=tuple(shaped(*dims, dtype=dtype) for dims, dtype in results),
-        in_specs=[WHOLE] * 3 + [anywhere] + [WHOLE] * 4 + [anywhere] + [WHOLE] * 2,
+        in_specs=[WHOLE] * 7 + [anywhere] + [WHOLE] * 4 + [anywhere] + [WHOLE] * 2,
         out_specs=(anywhere,) * len(results),
         scratch_shapes=kept[:1]
         + weights
@@ -773,7 +798,7 @@
         compiler_params=roomy(60, collective_id=0, has_side_effects=True),
         cost_estimate=busy(rows * states * width),
         name="mixer",
-    )(tokens, upstream, packed, in_weight, taps, select, step_weight, decay_log, out_weight, router, routes)
+    )(tokens, upstream, tap_bias, step_bias, skip, gain, second_gain, in_weight, taps, select, step_weight, decay_log, out_weight, router, routes)
 
 
 def mixer_back(
@@ -1153,16 +1178,17 @@
     here = sum_ref.at[pl.ds(4 * core, 4)]
     send(here, here, device(core=1 - core), (0, 0), 10).wait()
     whole = jnp.concatenate([sum_ref[q] for q in range(8)], axis=0)
-    last = jnp.concatenate([whole[112:120, k * LANES : (k + 1) * LANES] for k in range(whole.shape[1] // LANES)], axis=0)
+    last = [whole[112:120, k * LANES : (k + 1) * LANES] for k in range(whole.shape[1] // LANES)]
+    last = jnp.concatenate(last + [jnp.zeros((8, LANES), jnp.float32)], axis=0)
     narrow_out[...] = jnp.concatenate([whole[120:128], whole[108:112], whole[108:112]], axis=0)
     for c in range(2):
 
         @pl.when(core == c)
         def pick(c=c):
-            in_out[...] = whole[36 * c : 36 * c + 36]
+            in_out[...] = whole[36 * c : 36 * c + 40]
             out_out[...] = whole[72 + 18 * c : 90 + 18 * c]
-            left_out[...] = last[18 * c : 18 * c + 18]
-            right_out[...] = last[36 + 18 * c : 54 + 18 * c]
+            left_out[...] = last[18 * c : 18 * c + 24]
+            right_out[...] = last[36 + 18 * c : 60 + 18 * c]
 
 
 def start_halves(L, q, turn, source, halves, place, flip, device, send):
@@ -1188,7 +1214,7 @@
 
     return pl.pallas_call(
         shares_kernel,
-        out_shape=(shaped(36, width), shaped(18, width), shaped(18, LANES), shaped(18, LANES), shaped(16, width)),
+        out_shape=(shaped(40, width), shaped(18, width), shaped(24, LANES), shaped(24, LANES), shaped(16, width)),
         in_specs=[WHOLE] * 8,
         out_specs=(WHOLE,) * 5,
         scratch_shapes=[pltpu.VMEM((8, PIECE, width), jnp.float32)]
@@ -1200,6 +1226,58 @@
         compiler_params=roomy(60, collective_id=2, has_side_effects=True),
         name="shares",
     )(conv_cols, gate_cols, tokens, out_cols, middle, left, right, narrow)
+
+
+def finish_kernel(
+    in_ref, left_ref, right_ref, narrow_ref, expert_ref,
+    in_out, tap_out, tap_bias_out, select_out, step_out, step_bias_out, decay_out, skip_out, gain_out, second_out, router_out,
+    expert_first_out, expert_second_out,
+):
+    def turned(value):
+        size = value.shape[0]
+        same = lax.broadcasted_iota(jnp.int32, (size, size), 0) == lax.broadcasted_iota(jnp.int32, (size, size), 1)
+        ones = jnp.where(same, 1.0, 0.0).astype(jnp.bfloat16)
+        return sum(column_dot(part, ones) for part in three_parts(value))
+
+    each, taps, states = tap_out.shape[1], tap_out.shape[0], decay_out.shape[0]
+    in_out[...] = in_ref[: in_out.shape[0], :]
+    select_out[...] = left_ref[:each, : select_out.shape[1]]
+    sums = turned(left_ref[...])[SELECTED:, :each]
+    decay_out[...] = sums[:states]
+    tap_out[...] = sums[states : states + taps]
+    tap_bias_out[...] = sums[states + taps : states + taps + 1]
+    step_bias_out[...] = sums[states + taps + 1 : states + taps + 2]
+    skip_out[...] = sums[states + taps + 2 : states + taps + 3]
+    step_out[...] = right_ref[:each, : step_out.shape[1]]
+    fewer = router_out.shape[1]
+    owner = lax.axis_index("seq") * EXPERTS + lax.axis_index("expert")
+    shape = (narrow_ref.shape[1], LANES)
+    mine = lax.broadcasted_iota(jnp.int32, shape, 0) == lax.broadcasted_iota(jnp.int32, shape, 1) + owner * fewer
+    ones = jnp.where(mine, 1.0, 0.0).astype(jnp.bfloat16)
+    parts = three_parts(narrow_ref[...])
+    picked = sum(jnp.dot(part, ones, preferred_element_type=jnp.float32) for part in parts)
+    gain_out[...] = picked[EXPERTS : EXPERTS + 1, :fewer]
+    second_out[...] = picked[EXPERTS + 1 : EXPERTS + 2, :fewer]
+    router_out[...] = picked[:EXPERTS, :fewer]
+    expert_first_out[...] = expert_ref[0].astype(jnp.float32)
+    expert_second_out[...] = expert_ref[1].astype(jnp.float32)
+
+
+def finish(in_share, left, right, narrow, expert_share, devices, taps, states, rank, inner):
+    model = in_share.shape[1]
+    each, fewer, hidden = inner // devices, model // devices, expert_share.shape[1]
+    dims = (
+        (2 * each, model), (taps, each), (1, each), (each, rank + 2 * states), (each, rank), (1, each), (states, each), (1, each),
+        (1, fewer), (1, fewer), (EXPERTS, fewer), (hidden, model), (hidden, model),
+    )
+    return pl.pallas_call(
+        finish_kernel,
+        out_shape=tuple(shaped(*size) for size in dims),
+        in_specs=[WHOLE] * 5,
+        out_specs=(WHOLE,) * len(dims),
+        compiler_params=roomy(32),
+        name="finish",
+    )(in_share, left, right, narrow, expert_share)
 
 
 def local(
@@ -1222,30 +1300,26 @@
     expert_second,
 ):
     bf16, f32 = jnp.bfloat16, jnp.float32
-    stream = segmented(tokens[0])
-    routes = segmented(expert_index[0])
-    upstream = segmented(cotangent[0])
-    row_count, model_width = stream.shape
+    row_count, model_width = tokens.shape[1:]
     seat_count = 2 * row_count
     inner = conv_bias.shape[0]
     rank = step_weight.shape[0]
     states = decay_log.shape[0]
     taps = conv_weight.shape[0]
     seqs, experts = lax.axis_size("seq"), lax.axis_size("expert")
-    packed = jnp.concatenate([conv_bias, step_bias, skip_gain, first_gain, second_gain]).reshape(4, inner)
     (
         normed_in, gate_input, padded, preact, conv_out, step_raw, step_size, selection, first, mixer_out, gated,
-        middle, normed_mid, router_probs, gate_wide, leaving, slots, upstream_there,
+        middle, normed_mid, router_probs, gate_wide, leaving, slots, upstream_there, stream, upstream, packed,
     ) = mixer(
-        stream, upstream, packed, in_weight, conv_weight, select_weight, step_weight, decay_log, out_weight, router_weight, routes, seat_count
+        tokens[0], cotangent[0], conv_bias, step_bias, skip_gain, first_gain, second_gain, in_weight, conv_weight, select_weight.T, step_weight, decay_log, out_weight, router_weight.T, expert_index[:, :, 0], seat_count
     )
     back, value_there, expert_grads = expert_pass(leaving, upstream_there, expert_first[0], expert_second[0], seqs)
     expert_share = lax.psum_scatter(
         expert_grads.reshape(-1, model_width), "seq", scatter_dimension=0, tiled=True
     ).reshape(2, -1, model_width)
     middle_low, grad_gate_input, grad_conv_input, left, right, narrow, grad_tokens, value_home = mixer_back(
-        back, slots, router_probs, gate_wide, normed_mid, router_weight, middle, upstream, out_weight, gate_input, mixer_out, conv_out,
-        step_size, step_raw, selection, preact, padded, first, decay_log, step_weight, select_weight, conv_weight, packed, in_weight, stream, value_there,
+        back, slots, router_probs, gate_wide, normed_mid, router_weight.T, middle, upstream, out_weight, gate_input, mixer_out, conv_out,
+        step_size, step_raw, selection, preact, padded, first, decay_log, step_weight, select_weight.T, conv_weight, packed, in_weight, stream, value_there,
     )
     placing = (slots[:, 0:1] == jnp.arange(seat_count, dtype=f32)[None, :]).astype(bf16)
     mixed = middle + gate_wide[:, 0:1] * product(placing, value_home)
@@ -1255,26 +1329,26 @@
     in_share, out_share, left, right, narrow = shares(
         grad_conv_input, grad_gate_input, normed_in, gated, middle_low, left, right, narrow
     )
-    rows_sum = left[:, rank + 2 * states :]
-    owner = lax.axis_index("seq") * experts + lax.axis_index("expert")
-    narrow_sum = lax.dynamic_slice_in_dim(narrow, owner * fewer, fewer, axis=1)
+    in_grad, tap_grad, tap_bias_grad, select_grad, step_grad, step_bias_grad, decay_grad, skip_grad, gain_grad, second_grad, router_grad, first_grad, second_hidden = finish(
+        in_share, left, right, narrow, expert_share, devices, taps, states, rank, inner
+    )
     return (
         in_order(mixed.astype(bf16))[None],
-        in_order(grad_tokens)[None],
-        narrow_sum[0],
-        in_share.T,
-        rows_sum[:, states : states + taps].T,
-        rows_sum[:, states + taps],
-        left[:, : rank + 2 * states],
-        right[:, :rank].T,
-        rows_sum[:, states + taps + 1],
-        rows_sum[:, :states].T,
-        rows_sum[:, states + taps + 2],
+        grad_tokens[None],
+        gain_grad[0],
+        in_grad.T,
+        tap_grad,
+        tap_bias_grad[0],
+        select_grad,
+        step_grad.T,
+        step_bias_grad[0],
+        decay_grad,
+        skip_grad[0],
         out_share,
-        narrow_sum[1],
-        narrow_sum[2:10].T,
-        expert_share[0].T.astype(f32)[None],
-        expert_share[1].astype(f32)[None],
+        second_grad[0],
+        router_grad.T,
+        first_grad.T[None],
+        second_hidden[None],
     )
 
 

time: 317 us -> 304 us (0.959)
  local copies, waits for them, and re-layouts: 19 us -> 3.94 us
  Pallas kernels: 276 us -> 282 us
  other arithmetic: 3.17 us -> 0 us
    pallas_call x1, Pallas kernels: 91 us -> 94.7 us  [mixer_back(): pl.pallas_call(mixer_back_kernel, out_shape=tuple((shaped(*dims, dtype=dt...]
    transpose x4 -> x0, local copies, waits for them, and re-layouts: 3.54 us -> none  [the longest x1 1.38 us: local(): narrow_sum[2:10]]
    unnamed x48 -> x24, local copies, waits for them, and re-layouts: 6.42 us -> 2.92 us
    another operation x4 -> x0, local copies, waits for them, and re-layouts: 3.29 us -> none  [segmented(): block.reshape(SEGS, rows // SEGS, -1).transpose(1, 0, 2).reshape(rows, -1)]
    pallas_call x1 -> x2, Pallas kernels: 76.5 us -> 77.6 us  [the longest x1 76 us: shares(): pl.pallas_call(shares_kernel, out_shape=(shaped(40, width), shaped(18, wi...]
  transfers between devices with their start and end apart: 1 -> 1, of which waited for: 0 -> 0; matrix products, arithmetic and copies ran while one was open for 3% -> 1% of each run, Pallas kernels for 53% -> 57%
where the time goes in v2:
time: 304 us; the launch traced here: 301 us
  Pallas kernels  282 us (93%)
  between operations  14.4 us (5%)
  local copies, waits for them, and re-layouts  3.94 us (1%)
    pallas_call x1, Pallas kernels, mixer_back(): pl.pallas_call(mixer_back_kernel, out_shape=tuple((shaped(*dims, dtype=dt...  94.7 us
    pallas_call x1, Pallas kernels, shares(): pl.pallas_call(shares_kernel, out_shape=(shaped(40, width), shaped(18, wi...  76 us
    pallas_call x1, Pallas kernels, expert_pass(): pl.pallas_call(experts_kernel, out_shape=(shaped(rows, wide, dtype=bf16),...  57.8 us
    pallas_call x1, Pallas kernels, mixer(): pl.pallas_call(mixer_kernel, out_shape=tuple((shaped(*dims, dtype=dtype)...  51.5 us
  transfers between devices with their start and end apart: 1, of which 0 were waited for; matrix products, arithmetic and copies ran while one was open for 1% of the time, Pallas kernels for 57%

profile of v2, /device:TPU:1, one launch (start us, length us, event | category | flops | bytes accessed | tf_op | source)
XLA Modules:
  0.0 300.5 jit_solution(5024455050943430837)
XLA Ops:
  7.2 0.0 reduce-scatter.2.cloned.1.call-start
  7.2 51.5 %mixer.1 = (bf16[256,1152]{1,0:T(8,128)(2,1)}, f32[256,2304]{1,0:T(8,128)}, f32[280,2304]{1,0:T(8,128)}, f32[256,2304]{1,0:T(8,128)}, f32[256,2304]{1,0:T(8,128)...) custom-call(bf16[256,1152]{1,0:T(8,128)(2,1)} %bitcast.36, ...), custom_call_target="tpu_custom_call" | custom-call | flops 38654705664 | bytes 150994944 | tf_op jit(solution)/shard_map/mixer/pallas_call | solution.py:778
  58.8 57.8 %experts.1 = (bf16[512,1280]{1,0:T(8,128)(2,1)}, bf16[512,1152]{1,0:T(8,128)(2,1)}, bf16[16,2,192,1152]{3,2,1,0:T(8,128)(2,1)}) custom-call(bf16[512,1280]{1,0:T(8,128)(2,1)} %get-tuple-element.69.leaving_hbm, bf16[512,1152]{1,0:T(8,128)(2,1)} %get-tuple-element.70.up_ref, bf16[1152,3072]{1,0:T(8,128)(2,1)} %bitcast.32, bf16[3072,1152]{1,0:T(8,128)(2,1)} %bitcast.33), custom_call_target="tpu_custom_call" | custom-call | flops 21743271936 | bytes 28311552 | tf_op jit(solution)/shard_map/experts/pallas_call | solution.py:1016
  116.6 0.0 reduce-scatter.2.cloned.1.call-update
  116.6 94.7 %mixer_back.1 = (bf16[256,1152]{1,0:T(8,128)(2,1)}, bf16[256,2304]{1,0:T(8,128)(2,1)}, bf16[256,2304]{1,0:T(8,128)(2,1)}, f32[2304,128]{1,0:T(8,128)}, f32[2304,...) custom-call(bf16[512,1280]{1,0:T(8,128)(2,1)} %get-tuple-element.71.back_hbm, ...), custom_call_target="tpu_custom_call" | custom-call | flops 38654705664 | bytes 150994944 | tf_op jit(solution)/shard_map/mixer_back/pallas_call | solution.py:834
  211.3 0.0 copy-start.8
  211.3 0.0 copy-start.9
  211.3 0.0 copy-start.6
  211.3 76.0 %shares.1 = (f32[40,1152]{1,0:T(8,128)}, f32[18,1152]{1,0:T(8,128)}, f32[24,128]{1,0:T(8,128)}, f32[24,128]{1,0:T(8,128)}, f32[16,1152]{1,0:T(8,128)}) custom-call(bf16[256,2304]{1,0:T(8,128)(2,1)} %get-tuple-element.89.conv_cols, bf16[256,2304]{1,0:T(8,128)(2,1)} %get-tuple-element.90.gate_cols, bf16[256,1152]{1,0:T(8,128)(2,1)} %get-tuple-element.91.token_ref, ...), custom_call_target="tpu_custom_call" | custom-call | tf_op jit(solution)/shard_map/shares/pallas_call | solution.py:1215
  287.4 0.0 copy-done.8
  287.4 0.0 copy-done.9
  287.4 0.1 slice_reduce_fusion
  287.5 0.0 copy-done.7
  287.5 0.0 copy-start.5
  287.5 0.5 fusion.2
  288.1 0.9 copy.34
  289.0 0.0 copy-done.1
  289.0 0.1 copy-done.2
  289.1 0.0 copy-done.3
  289.1 1.2 copy-done
  290.3 1.6 finish.1
  291.8 0.0 copy-done.5
  291.8 1.0 copy.37
  292.8 0.6 copy.38
  (11 shorter events, 0.0 us)
Async XLA Ops:
  7.2 281.8 %reduce-scatter.2.cloned.1.call-start = ((), (), s32[]{:S(2)}) async-start(), calls=%async_computation.1 | async-start | bytes 15040512 | tf_op jit(solution)/shard_map/reduce_scatter | solution.py:1317
  211.3 76.1 %copy-start.8 = (f32[256,128]{1,0:T(8,128)S(1)}, f32[256,128]{1,0:T(8,128)}, u32[]{:S(2)}) copy-start(f32[256,128]{1,0:T(8,128)} %get-tuple-element.67.chosen_ref) | copy-start | bytes 393220
  211.3 76.1 %copy-start.9 = (f32[256,128]{1,0:T(8,128)S(1)}, f32[256,128]{1,0:T(8,128)}, u32[]{:S(2)}) copy-start(f32[256,128]{1,0:T(8,128)} %get-tuple-element.68.slot_ref) | copy-start | bytes 393220
  211.3 76.2 %copy-start.6 = (f32[256,1152]{1,0:T(8,128)S(1)}, f32[256,1152]{1,0:T(8,128)}, u32[]{:S(2)}) copy-start(f32[256,1152]{1,0:T(8,128)} %get-tuple-element.66.middle_ref) | copy-start | bytes 3538948
  211.3 76.2 %copy-start.7 = (bf16[512,1152]{1,0:T(8,128)(2,1)S(1)}, bf16[512,1152]{1,0:T(8,128)(2,1)}, u32[]{:S(2)}) copy-start(bf16[512,1152]{1,0:T(8,128)(2,1)} %get-tuple-element.87) | copy-start | bytes 3538948
  287.5 4.3 %copy-start.5 = (f32[256,1152]{1,0:T(8,128)S(1)}, f32[256,1152]{1,0:T(8,128)}, u32[]{:S(2)}) copy-start(f32[256,1152]{1,0:T(8,128)} %get-tuple-element.88) | copy-start | bytes 3538948
  288.1 0.9 copy-start.1
  288.1 1.0 copy-start.2
  288.1 1.0 copy-start.3
  288.1 1.0 copy-start.4
  289.1 1.2 copy-start
  291.8 1.0 copy-start.10
Sparse Core Ops, SparseCore 0:
  116.7 101.0 reduce-scatter.1

commit v3 on v2

--- a/solution.py
+++ b/solution.py
@@ -96,7 +96,7 @@
             return span + step, memory
 
         zero = jnp.zeros((SEGS, LANES), jnp.float32)
-        span, memory = lax.fori_loop(0, steps, advance, (zero, jnp.zeros(rate.shape, jnp.float32)), unroll=8)
+        span, memory = lax.fori_loop(0, steps, advance, (zero, jnp.zeros(rate.shape, jnp.float32)), unroll=16)
         hop = 1
         while hop < SEGS:
             memory = memory + jnp.exp2(rate * span) * neighbour(memory, hop, later, 0.0)
@@ -142,7 +142,7 @@
             y_ref[rows_of(j), lanes] = jnp.sum(wide_out[j] * memory, axis=0)
             return memory
 
-        lax.fori_loop(0, steps, advance, first, unroll=8)
+        lax.fori_loop(0, steps, advance, first, unroll=16)
         return unused
 
     lax.fori_loop(0, blocks, block, 0)
@@ -190,7 +190,7 @@
             return mu, slow + kept * step
 
         last = entering(True, part_ref, span_ref, rate, lanes, carried_at(in_ref, part, i))
-        unused_mu, slow = lax.fori_loop(0, steps, retreat, (last, jnp.zeros(rate.shape, jnp.float32)), unroll=4)
+        unused_mu, slow = lax.fori_loop(0, steps, retreat, (last, jnp.zeros(rate.shape, jnp.float32)), unroll=8)
         glog_ref[:, lanes] = (1.0 / LOG2E) * jnp.sum(slow * rate, axis=1)
         raw_steps = raw_rows[...]
         gbias_ref[:, lanes] = jnp.sum(raw_steps, axis=0, keepdims=True)
@@ -1047,6 +1047,7 @@
 
 ORDERS = ("xyz", "yzx", "zxy")
 PIECE = 16
+TURNS = (0, 2, 1, 3)
 
 
 def shares_kernel(
@@ -1057,7 +1058,7 @@
     core = lax.rem(expert, 2)
     place = {"y": lax.div(seq, 4), "z": lax.rem(seq, 4), "x": lax.div(expert, 2)}
     third = token_ref.shape[1] // len(ORDERS)
-    streams = [(L, q) for L in range(len(ORDERS)) for q in range(4)]
+    streams = [(L, q) for q in TURNS for L in range(len(ORDERS))]
 
     def flip(i):
         return i + 1 - 2 * lax.rem(i, 2)
@@ -1104,7 +1105,7 @@
     pending, holding = {}, {}
 
     def set_out(L):
-        for q in range(4):
+        for q in TURNS:
             for copy in pending[L, q]:
                 copy.wait()
             add(taken.at[L, q], made.at[L, 4 * core + q], 64)
@@ -1143,7 +1144,7 @@
             return unused
 
         lax.fori_loop(0, 16, block, 0, unroll=2)
-        for q in range(4):
+        for q in TURNS:
             pending[L, q] = [
                 send(made.at[L, 4 * (1 - core) + q], taken.at[L, q], device(core=1 - core), (L, q), 0)
             ]

time: 304 us -> 292 us (0.961)
  Pallas kernels: 282 us -> 268 us
    pallas_call x1, Pallas kernels: 94.7 us -> 82.4 us  [mixer_back(): pl.pallas_call(mixer_back_kernel, out_shape=tuple((shaped(*dims, dtype=dt...]
  transfers between devices with their start and end apart: 1 -> 1, of which waited for: 0 -> 0; matrix products, arithmetic and copies ran while one was open for 1% -> 1% of each run, Pallas kernels for 57% -> 55%
where the time goes in v3:
time: 292 us; the launch traced here: 288 us
  Pallas kernels  268 us (92%)
  between operations  14.5 us (5%)
  local copies, waits for them, and re-layouts  3.94 us (1%)
    pallas_call x1, Pallas kernels, mixer_back(): pl.pallas_call(mixer_back_kernel, out_shape=tuple((shaped(*dims, dtype=dt...  82.4 us
    pallas_call x1, Pallas kernels, shares(): pl.pallas_call(shares_kernel, out_shape=(shaped(40, width), shaped(18, wi...  75.1 us
    pallas_call x1, Pallas kernels, expert_pass(): pl.pallas_call(experts_kernel, out_shape=(shaped(rows, wide, dtype=bf16),...  58 us
    pallas_call x1, Pallas kernels, mixer(): pl.pallas_call(mixer_kernel, out_shape=tuple((shaped(*dims, dtype=dtype)...  51.4 us
  transfers between devices with their start and end apart: 1, of which 0 were waited for; matrix products, arithmetic and copies ran while one was open for 1% of the time, Pallas kernels for 55%

profile of v3, /device:TPU:1, one launch (start us, length us, event | category | flops | bytes accessed | tf_op | source)
XLA Modules:
  0.0 287.5 jit_solution(1458269525732876651)
XLA Ops:
  7.2 0.0 reduce-scatter.2.cloned.1.call-start
  7.2 51.4 %mixer.1 = (bf16[256,1152]{1,0:T(8,128)(2,1)}, f32[256,2304]{1,0:T(8,128)}, f32[280,2304]{1,0:T(8,128)}, f32[256,2304]{1,0:T(8,128)}, f32[256,2304]{1,0:T(8,128)...) custom-call(bf16[256,1152]{1,0:T(8,128)(2,1)} %bitcast.36, ...), custom_call_target="tpu_custom_call" | custom-call | flops 38654705664 | bytes 150994944 | tf_op jit(solution)/shard_map/mixer/pallas_call | solution.py:778
  58.7 58.0 %experts.1 = (bf16[512,1280]{1,0:T(8,128)(2,1)}, bf16[512,1152]{1,0:T(8,128)(2,1)}, bf16[16,2,192,1152]{3,2,1,0:T(8,128)(2,1)}) custom-call(bf16[512,1280]{1,0:T(8,128)(2,1)} %get-tuple-element.69.leaving_hbm, bf16[512,1152]{1,0:T(8,128)(2,1)} %get-tuple-element.70.up_ref, bf16[1152,3072]{1,0:T(8,128)(2,1)} %bitcast.32, bf16[3072,1152]{1,0:T(8,128)(2,1)} %bitcast.33), custom_call_target="tpu_custom_call" | custom-call | flops 21743271936 | bytes 28311552 | tf_op jit(solution)/shard_map/experts/pallas_call | solution.py:1016
  116.6 0.0 reduce-scatter.2.cloned.1.call-update
  116.7 82.4 %mixer_back.1 = (bf16[256,1152]{1,0:T(8,128)(2,1)}, bf16[256,2304]{1,0:T(8,128)(2,1)}, bf16[256,2304]{1,0:T(8,128)(2,1)}, f32[2304,128]{1,0:T(8,128)}, f32[2304,...) custom-call(bf16[512,1280]{1,0:T(8,128)(2,1)} %get-tuple-element.71.back_hbm, ...), custom_call_target="tpu_custom_call" | custom-call | flops 38654705664 | bytes 150994944 | tf_op jit(solution)/shard_map/mixer_back/pallas_call | solution.py:834
  199.1 0.0 copy-start.8
  199.1 0.0 copy-start.9
  199.1 0.0 copy-start.6
  199.2 0.0 copy-start.7
  199.2 75.1 %shares.1 = (f32[40,1152]{1,0:T(8,128)}, f32[18,1152]{1,0:T(8,128)}, f32[24,128]{1,0:T(8,128)}, f32[24,128]{1,0:T(8,128)}, f32[16,1152]{1,0:T(8,128)}) custom-call(bf16[256,2304]{1,0:T(8,128)(2,1)} %get-tuple-element.89.conv_cols, bf16[256,2304]{1,0:T(8,128)(2,1)} %get-tuple-element.90.gate_cols, bf16[256,1152]{1,0:T(8,128)(2,1)} %get-tuple-element.91.token_ref, ...), custom_call_target="tpu_custom_call" | custom-call | tf_op jit(solution)/shard_map/shares/pallas_call | solution.py:1216
  274.3 0.1 slice_reduce_fusion
  274.4 0.0 copy-done.7
  274.4 0.0 copy-start.5
  274.4 0.6 fusion.2
  275.0 0.0 copy-start.1
  275.0 0.0 copy-start.2
  275.0 0.0 copy-start.3
  275.0 0.9 copy.34
  275.9 0.0 copy-done.1
  275.9 0.1 copy-done.2
  276.0 1.2 copy-done
  277.2 1.6 finish.1
  278.7 1.0 copy.37
  279.7 0.6 copy.38
  (11 shorter events, 0.0 us)
Async XLA Ops:
  7.2 268.7 %reduce-scatter.2.cloned.1.call-start = ((), (), s32[]{:S(2)}) async-start(), calls=%async_computation.1 | async-start | bytes 15040512 | tf_op jit(solution)/shard_map/reduce_scatter | solution.py:1318
  199.1 75.1 %copy-start.8 = (f32[256,128]{1,0:T(8,128)S(1)}, f32[256,128]{1,0:T(8,128)}, u32[]{:S(2)}) copy-start(f32[256,128]{1,0:T(8,128)} %get-tuple-element.67.chosen_ref) | copy-start | bytes 393220
  199.1 75.1 %copy-start.9 = (f32[256,128]{1,0:T(8,128)S(1)}, f32[256,128]{1,0:T(8,128)}, u32[]{:S(2)}) copy-start(f32[256,128]{1,0:T(8,128)} %get-tuple-element.68.slot_ref) | copy-start | bytes 393220
  199.1 75.3 %copy-start.6 = (f32[256,1152]{1,0:T(8,128)S(1)}, f32[256,1152]{1,0:T(8,128)}, u32[]{:S(2)}) copy-start(f32[256,1152]{1,0:T(8,128)} %get-tuple-element.66.middle_ref) | copy-start | bytes 3538948
  199.2 75.3 %copy-start.7 = (bf16[512,1152]{1,0:T(8,128)(2,1)S(1)}, bf16[512,1152]{1,0:T(8,128)(2,1)}, u32[]{:S(2)}) copy-start(bf16[512,1152]{1,0:T(8,128)(2,1)} %get-tuple-element.87) | copy-start | bytes 3538948
  274.4 4.3 %copy-start.5 = (f32[256,1152]{1,0:T(8,128)S(1)}, f32[256,1152]{1,0:T(8,128)}, u32[]{:S(2)}) copy-start(f32[256,1152]{1,0:T(8,128)} %get-tuple-element.88) | copy-start | bytes 3538948
  275.0 0.9 copy-start.1
  275.0 1.0 copy-start.2
  275.0 1.0 copy-start.3
  275.0 1.0 copy-start.4
  276.0 1.2 copy-start
  278.7 1.0 copy-start.10
Sparse Core Ops, SparseCore 0:
  116.8 100.9 reduce-scatter.1

commit v4 on v3

--- a/solution.py
+++ b/solution.py
@@ -914,7 +914,7 @@
 
 def experts_kernel(
     leaving_hbm, up_ref, first_hbm, second_hbm, back_out, value_out, sums_out,
-    received, first, second, pull, active, grad, value, sent, back, scaled_received, scaled_up, staged_sums,
+    received, first, second, pull, active, grad, value, sent, dots, scaled_received, scaled_up, staged_sums,
     loads, saves, goes, comes, returns, arrives,
 ):
     rows, width = up_ref.shape
@@ -942,6 +942,8 @@
     for copy in arriving:
         copy.wait()
 
+    dots[...] = jnp.zeros_like(dots)
+
     def layer(i, unused):
         cols = pl.ds(pl.multiple_of(i * CHUNK, CHUNK), CHUNK)
         pre = jnp.dot(received[:, :width], first[:, cols], preferred_element_type=jnp.float32)
@@ -949,23 +951,27 @@
         bent = jnp.tanh(pre * (GELU_OUT + GELU_OUT * GELU_IN * square))
         share = 0.5 + 0.5 * bent
         slope = share + pre * (0.5 - 0.5 * bent * bent) * (GELU_OUT + 3.0 * GELU_OUT * GELU_IN * square)
-        active[:, cols] = (pre * share).astype(jnp.bfloat16)
-        grad[:, cols] = (slope * pull[:, cols].astype(jnp.float32)).astype(jnp.bfloat16)
+        low = (pre * share).astype(jnp.bfloat16)
+        active[:, cols] = low
+        drawn = pull[:, cols].astype(jnp.float32)
+        grad[:, cols] = (slope * drawn).astype(jnp.bfloat16)
+        met = low.astype(jnp.float32) * drawn
+        dots[...] += sum(met[:, k * LANES : (k + 1) * LANES] for k in range(CHUNK // LANES))
         return unused
 
     lax.fori_loop(0, hidden // CHUNK, layer, 0)
-    value[...] = jnp.dot(active[...], second[...], preferred_element_type=jnp.float32).astype(jnp.bfloat16)
-    saving = [pltpu.make_async_copy(value, value_out, saves.at[0])]
-    saving[0].start()
     sent[:, :width] = transposed_dot(grad[...], first[...]).astype(jnp.bfloat16)
-    along = jnp.sum(value[...].astype(jnp.float32) * up_ref[...].astype(jnp.float32), axis=1, keepdims=True)
+    along = jnp.sum(dots[...], axis=1, keepdims=True)
     place = lax.broadcasted_iota(jnp.int32, (rows, LANES), 1)
     tail = jnp.zeros(place.shape, jnp.float32)
     for k, part in enumerate(three_parts(along)):
         tail = jnp.where(place == k, part.astype(jnp.float32), tail)
     sent[:, width:] = tail.astype(jnp.bfloat16)
-    returning = trade(sent, back, returns, arrives)
-
+    returning = trade(sent, back_out, returns, arrives)
+
+    value[...] = jnp.dot(active[...], second[...], preferred_element_type=jnp.float32).astype(jnp.bfloat16)
+    saving = [pltpu.make_async_copy(value, value_out, saves.at[0])]
+    saving[0].start()
     parts = received[:, width:].astype(jnp.float32)
     gate = parts[:, 0:1] + parts[:, 1:2] + parts[:, 2:3]
     scaled_received[...] = (received[:, :width].astype(jnp.float32) * gate).astype(jnp.bfloat16)
@@ -996,9 +1002,6 @@
         stored(i, i % 2).wait()
     for copy in returning:
         copy.wait()
-    last = pltpu.make_async_copy(back, back_out, saves.at[3])
-    last.start()
-    last.wait()
     saving[0].wait()
 
 
@@ -1031,12 +1034,12 @@
             kept(rows, hidden),
             kept(rows, width),
             kept(rows, wide),
-            kept(rows, wide),
+            pltpu.VMEM((rows, LANES), jnp.float32),
             kept(rows, width),
             kept(rows, width),
             kept(2, 2, 2, half, width),
             pltpu.SemaphoreType.DMA((2,)),
-            pltpu.SemaphoreType.DMA((4,)),
+            pltpu.SemaphoreType.DMA((3,)),
         ]
         + [pltpu.SemaphoreType.DMA((EXPERTS,))] * 4,
         compiler_params=roomy(60, collective_id=3, has_side_effects=True),

time: 292 us -> 290 us (level)
  no operation moved by 1% of the time
where the time goes in v4:
time: 290 us; the launch traced here: 285 us
  Pallas kernels  266 us (92%)
  between operations  14.5 us (5%)
  local copies, waits for them, and re-layouts  3.94 us (1%)
    pallas_call x1, Pallas kernels, mixer_back(): pl.pallas_call(mixer_back_kernel, out_shape=tuple((shaped(*dims, dtype=dt...  82.8 us
    pallas_call x1, Pallas kernels, shares(): pl.pallas_call(shares_kernel, out_shape=(shaped(40, width), shaped(18, wi...  74.9 us
    pallas_call x1, Pallas kernels, expert_pass(): pl.pallas_call(experts_kernel, out_shape=(shaped(rows, wide, dtype=bf16),...  55.6 us
    pallas_call x1, Pallas kernels, mixer(): pl.pallas_call(mixer_kernel, out_shape=tuple((shaped(*dims, dtype=dtype)...  51.4 us
  transfers between devices with their start and end apart: 1, of which 0 were waited for; matrix products, arithmetic and copies ran while one was open for 1% of the time, Pallas kernels for 55%

profile of v4, /device:TPU:1, one launch (start us, length us, event | category | flops | bytes accessed | tf_op | source)
XLA Modules:
  0.0 285.4 jit_solution(10662251543563514467)
XLA Ops:
  7.2 0.0 reduce-scatter.2.cloned.1.call-start
  7.2 51.4 %mixer.1 = (bf16[256,1152]{1,0:T(8,128)(2,1)}, f32[256,2304]{1,0:T(8,128)}, f32[280,2304]{1,0:T(8,128)}, f32[256,2304]{1,0:T(8,128)}, f32[256,2304]{1,0:T(8,128)...) custom-call(bf16[256,1152]{1,0:T(8,128)(2,1)} %bitcast.36, ...), custom_call_target="tpu_custom_call" | custom-call | flops 38654705664 | bytes 150994944 | tf_op jit(solution)/shard_map/mixer/pallas_call | solution.py:778
  58.7 55.6 %experts.1 = (bf16[512,1280]{1,0:T(8,128)(2,1)}, bf16[512,1152]{1,0:T(8,128)(2,1)}, bf16[16,2,192,1152]{3,2,1,0:T(8,128)(2,1)}) custom-call(bf16[512,1280]{1,0:T(8,128)(2,1)} %get-tuple-element.69.leaving_hbm, bf16[512,1152]{1,0:T(8,128)(2,1)} %get-tuple-element.70.up_ref, bf16[1152,3072]{1,0:T(8,128)(2,1)} %bitcast.32, bf16[3072,1152]{1,0:T(8,128)(2,1)} %bitcast.33), custom_call_target="tpu_custom_call" | custom-call | flops 21743271936 | bytes 28311552 | tf_op jit(solution)/shard_map/experts/pallas_call | solution.py:1019
  114.3 0.0 reduce-scatter.2.cloned.1.call-update
  114.3 82.8 %mixer_back.1 = (bf16[256,1152]{1,0:T(8,128)(2,1)}, bf16[256,2304]{1,0:T(8,128)(2,1)}, bf16[256,2304]{1,0:T(8,128)(2,1)}, f32[2304,128]{1,0:T(8,128)}, f32[2304,...) custom-call(bf16[512,1280]{1,0:T(8,128)(2,1)} %get-tuple-element.71.back_hbm, ...), custom_call_target="tpu_custom_call" | custom-call | flops 38654705664 | bytes 150994944 | tf_op jit(solution)/shard_map/mixer_back/pallas_call | solution.py:834
  197.2 0.0 copy-start.8
  197.2 0.0 copy-start.9
  197.2 0.0 copy-start.6
  197.2 0.0 copy-start.7
  197.2 74.9 %shares.1 = (f32[40,1152]{1,0:T(8,128)}, f32[18,1152]{1,0:T(8,128)}, f32[24,128]{1,0:T(8,128)}, f32[24,128]{1,0:T(8,128)}, f32[16,1152]{1,0:T(8,128)}) custom-call(bf16[256,2304]{1,0:T(8,128)(2,1)} %get-tuple-element.89.conv_cols, bf16[256,2304]{1,0:T(8,128)(2,1)} %get-tuple-element.90.gate_cols, bf16[256,1152]{1,0:T(8,128)(2,1)} %get-tuple-element.91.token_ref, ...), custom_call_target="tpu_custom_call" | custom-call | tf_op jit(solution)/shard_map/shares/pallas_call | solution.py:1219
  272.1 0.1 slice_reduce_fusion
  272.3 0.0 copy-done.6
  272.3 0.6 fusion.2
  272.9 0.0 copy-start.1
  272.9 0.0 copy-start.2
  272.9 0.0 copy-start.3
  272.9 0.0 copy-start.4
  272.9 0.9 copy.34
  273.8 0.0 copy-done.1
  273.8 0.1 copy-done.2
  273.8 1.2 copy-done
  275.0 1.6 finish.1
  276.6 1.0 copy.37
  277.6 0.6 copy.38
  (11 shorter events, 0.0 us)
Async XLA Ops:
  7.2 266.6 %reduce-scatter.2.cloned.1.call-start = ((), (), s32[]{:S(2)}) async-start(), calls=%async_computation.1 | async-start | bytes 15040512 | tf_op jit(solution)/shard_map/reduce_scatter | solution.py:1321
  197.2 75.0 %copy-start.8 = (f32[256,128]{1,0:T(8,128)S(1)}, f32[256,128]{1,0:T(8,128)}, u32[]{:S(2)}) copy-start(f32[256,128]{1,0:T(8,128)} %get-tuple-element.67.chosen_ref) | copy-start | bytes 393220
  197.2 75.0 %copy-start.9 = (f32[256,128]{1,0:T(8,128)S(1)}, f32[256,128]{1,0:T(8,128)}, u32[]{:S(2)}) copy-start(f32[256,128]{1,0:T(8,128)} %get-tuple-element.68.slot_ref) | copy-start | bytes 393220
  197.2 75.1 %copy-start.6 = (f32[256,1152]{1,0:T(8,128)S(1)}, f32[256,1152]{1,0:T(8,128)}, u32[]{:S(2)}) copy-start(f32[256,1152]{1,0:T(8,128)} %get-tuple-element.66.middle_ref) | copy-start | bytes 3538948
  197.2 75.1 %copy-start.7 = (bf16[512,1152]{1,0:T(8,128)(2,1)S(1)}, bf16[512,1152]{1,0:T(8,128)(2,1)}, u32[]{:S(2)}) copy-start(bf16[512,1152]{1,0:T(8,128)(2,1)} %get-tuple-element.87) | copy-start | bytes 3538948
  272.3 4.3 %copy-start.5 = (f32[256,1152]{1,0:T(8,128)S(1)}, f32[256,1152]{1,0:T(8,128)}, u32[]{:S(2)}) copy-start(f32[256,1152]{1,0:T(8,128)} %get-tuple-element.88) | copy-start | bytes 3538948
  272.9 0.9 copy-start.1
  272.9 1.0 copy-start.2
  272.9 1.0 copy-start.3
  272.9 1.0 copy-start.4
  273.8 1.2 copy-start
  276.6 1.0 copy-start.10
Sparse Core Ops, SparseCore 0:
  114.4 101.1 reduce-scatter.1
